TPU v7x, 256 devices: a whole 4x4x8 slice. The times are simulated.
256 devices in a mesh: section: 2 (over core), tile: 32 (over y, z), wave: 4 (over x).
Axes of the slice: x: 4, y: 4, z: 8, core: 2. Of those that a mesh axis runs over, the one named last changes fastest.
Arguments:
- rf_rows: bfloat16 [8, 64, 1024, 2048], P('wave', None, ('section', 'tile')), may hold values from -14 to 14
- filter_taps: bfloat16 [128], replicated, may hold values from -0.5 to 0.5
- interp_weights: bfloat16 [64, 16, 2048, 128], P(('section', 'tile')), may hold values from -0.125 to 0.125
- apodization: float32 [8, 32, 128], P('wave'), may hold values from 0.1 to 1
- fanout: int32 [64, 16], P(('section', 'tile')), may hold values from 0 to 31, as said below
- live_slots: int32 [64], P(('section', 'tile')), may hold values from 1 to 16, as said below
- offsets: int32 [64, 16, 8], P(('section', 'tile'), None, 'wave'), may hold values from 128 to 1920
- owned_tiles: int32 [32], replicated, may hold values from 0 to 31, each once
Outputs:
- doppler: float32 [32, 128], P('tile')
Inputs may be any that keep to these rules, and one draw needn't show every extreme that they name: `fanout`: each row names 16 different voxel tiles; row b begins with b % 32. Element tile b feeds the voxel tiles of the first live_slots[b] entries of its fanout row; later entries are unused. Some element tile has all 16 live.
All inputs are finite; a program needn't handle non-finite values.
Results may differ from a plain program's by a relative error of at most 0.0022.
Values sent between devices are 32-bit elements; how exact they have to be, the bound alone decides.
No kernel may reach another device: no remote copies, remote signals or barrier semaphores. Data moves between devices by JAX's collectives and lax.ppermute only.
A program may use at most 64 MiB of HBM per device.

v0:
```python
import jax
import jax.numpy as jnp
from jax import lax
from jax.sharding import PartitionSpec as P


def toeplitz_table(filter_taps, window, history):
    width = 2 * window + history
    padded = jnp.concatenate([jnp.zeros((width - history,), filter_taps.dtype), filter_taps])
    height = window + history
    flat = jnp.tile(padded, height)[: height * (width - 1)]
    return flat.reshape(height, width - 1)[:, :window]


def on_device(
    rf_rows, filter_taps, interp_weights, apodization, fanout, live_slots, offsets, owned_tiles
):
    wave_count, frame_count, tile_elems, sample_count = rf_rows.shape
    history = filter_taps.shape[0]
    slot_count = interp_weights.shape[1]
    window = interp_weights.shape[2] // tile_elems
    voxels = interp_weights.shape[3]
    toeplitz = toeplitz_table(filter_taps, window, history)

    def slot_step(slot_index, compact):
        segments = jnp.stack(
            [
                lax.dynamic_slice_in_dim(
                    rf_rows[wave_index],
                    offsets[0, slot_index, wave_index] - history,
                    window + history,
                    2,
                )
                for wave_index in range(wave_count)
            ]
        )
        filtered = jnp.einsum(
            "wfet,ts->wfes", segments, toeplitz, preferred_element_type=jnp.float32
        ).astype(jnp.bfloat16)
        beam = jnp.dot(
            filtered.reshape(wave_count * frame_count, tile_elems * window),
            interp_weights[0, slot_index],
            preferred_element_type=jnp.float32,
        ).reshape(wave_count, frame_count, voxels)
        wave_weights = lax.dynamic_index_in_dim(
            apodization, fanout[0, slot_index], 1, keepdims=False
        )
        term = jnp.sum(wave_weights[:, None, :] * beam, axis=0)
        return lax.dynamic_update_index_in_dim(compact, term, slot_index, 0)

    compact = lax.fori_loop(
        0, live_slots[0], slot_step, jnp.zeros((slot_count, frame_count, voxels), jnp.float32)
    )
    live_mask = jnp.arange(slot_count) < live_slots[0]
    routing = ((fanout[0][:, None] == owned_tiles[None, :]) & live_mask[:, None]).astype(
        jnp.float32
    )
    owner_part = lax.psum_scatter(
        jnp.einsum("kt,kfx->tfx", routing, compact, precision=lax.Precision.HIGHEST),
        "tile",
        scatter_dimension=0,
        tiled=True,
    )
    image_sum = lax.psum(owner_part[0], ("section", "wave"))
    clutter = jnp.mean(image_sum, axis=0, keepdims=True)
    deviation = image_sum - clutter
    return jnp.mean(deviation * deviation, axis=0)[None]


def solution(mesh):
    return jax.shard_map(
        on_device,
        mesh=mesh,
        in_specs=(
            P("wave", None, ("section", "tile"), None),
            P(),
            P(("section", "tile"), None, None, None),
            P("wave", None, None),
            P(("section", "tile"), None),
            P(("section", "tile")),
            P(("section", "tile"), None, "wave"),
            P(),
        ),
        out_specs=P("tile", None),
        check_vma=False,
    )
```

profile of v0, /device:TPU:1, one launch (start us, length us, event | category | flops | bytes accessed | tf_op | source)
XLA Modules:
  0.0 486.1 jit_solution(5102439698821190283)
XLA Ops:
  8.5 225.6 %while.15 = (s32[]{:T(128)}, f32[16,64,128]{2,0,1:T(8,128)S(1)}, s32[]{:T(128)}, s32[1,16]{1,0:T(1,128)}, f32[2,32,128]{2,1,0:T(8,128)}, /*index=5*/bf16[2,64,16...) while((s32[]{:T(128)}, f32[16,64,128]{2,0,1:T(8,128)S(1)}, ...), condition=%wide.region_2.3_spmd, body=%wide.region_0.2_spmd.sunk | while | flops 202137616 | bytes 22711924 | solution.py:51
  9.2 1.4 constant_dynamic-slice_fusion.10
  13.0 4.0 fusion.29
  21.1 1.3 fusion.30
  23.3 1.4 constant_dynamic-slice_fusion.10
  27.0 4.0 fusion.29
  35.2 1.3 fusion.30
  37.3 1.4 constant_dynamic-slice_fusion.10
  41.1 4.0 fusion.29
  49.2 1.3 fusion.30
  51.4 1.4 constant_dynamic-slice_fusion.10
  55.1 4.0 fusion.29
  63.3 1.3 fusion.30
  65.4 1.4 constant_dynamic-slice_fusion.10
  69.2 4.0 fusion.29
  77.4 1.3 fusion.30
  79.5 1.4 constant_dynamic-slice_fusion.10
  83.3 4.0 fusion.29
  91.4 1.3 fusion.30
  93.6 1.4 constant_dynamic-slice_fusion.10
  97.3 4.0 fusion.29
  105.5 1.3 fusion.30
  107.6 1.4 constant_dynamic-slice_fusion.10
  111.4 4.0 fusion.29
  119.5 1.3 fusion.30
  121.7 1.4 constant_dynamic-slice_fusion.10
  125.4 4.0 fusion.29
  135.7 1.4 constant_dynamic-slice_fusion.10
  139.5 4.0 fusion.29
  147.6 1.3 fusion.30
  149.8 1.4 constant_dynamic-slice_fusion.10
  153.6 4.0 fusion.29
  163.8 1.4 constant_dynamic-slice_fusion.10
  167.6 4.0 fusion.29
  177.9 1.4 constant_dynamic-slice_fusion.10
  181.7 4.0 fusion.29
  189.8 1.3 fusion.30
  191.9 1.4 constant_dynamic-slice_fusion.10
  195.7 4.0 fusion.29
  203.8 1.3 fusion.30
  206.0 1.4 constant_dynamic-slice_fusion.10
  209.8 4.0 fusion.29
  220.0 1.4 constant_dynamic-slice_fusion.10
  223.8 4.0 fusion.29
  234.1 1.3 fusion.9
  235.5 1.6 copy.13
  237.1 209.2 %reduce-scatter.2.cloned.1.call-done = f32[1,64,128]{2,1,0:T(8,128)} async-done(((f32[32,64,128]{2,1,0:T(8,128)}), f32[1,64,128]{2,1,0:T(8,128)}) %reduce-scatter.2.cloned.1.call-update) | async-done | bytes 32784 | tf_op jit(solution)/shard_map/reduce_scatter | solution.py:58
  446.3 32.4 %psum.7 = f32[64,128]{1,0:T(8,128)S(1)} all-reduce(f32[64,128]{1,0:T(8,128)} %bitcast.58), channel_id=1, replica_groups=mesh['section'=2,'tile'=32,'wave'=4] {'section','wave'}, use_global_device_ids=true, to_apply=%region_4.5 | all-reduce | flops 8192 | bytes 65536 | tf_op jit(solution)/shard_map/psum | solution.py:64
  (148 shorter events, 49.4 us)
Async XLA Ops:
  6.5 439.7 %reduce-scatter.2.cloned.1.call-start = ((), (), s32[]{:S(2)}) async-start(), calls=%async_computation.1 | async-start | bytes 1081344 | tf_op jit(solution)/shard_map/reduce_scatter | solution.py:58
  8.5 225.6 %copy-start.1 = (s32[32]{0:T(128)S(1)}, s32[32]{0:T(128)}, u32[]{:S(2)}) copy-start(s32[32]{0:T(128)} %param.17) | copy-start | bytes 388
  17.0 1.1 copy-start
  31.0 1.2 copy-start
  45.1 1.1 copy-start
  59.2 1.1 copy-start
  73.2 1.2 copy-start
  87.3 1.1 copy-start
  101.3 1.1 copy-start
  115.4 1.1 copy-start
  129.5 1.1 copy-start
  143.5 1.1 copy-start
  157.6 1.1 copy-start
  171.6 1.1 copy-start
  185.7 1.1 copy-start
  199.7 1.1 copy-start
  213.8 1.1 copy-start
  227.8 1.1 copy-start
Sparse Core Ops, SparseCore 0:
  237.2 209.0 reduce-scatter.1
where the time goes:
time: 489 us; the launch traced here: 486 us
  waiting for transfers between devices  209 us (43%)
  local copies, waits for them, and re-layouts  123 us (25%)
  loops' own time  77.4 us (16%)
  blocking collectives  32.4 us (7%)
  matrix products  29.5 us (6%)
  between operations  14.1 us (3%)
    reduce_scatter x1, waiting for transfers between devices, on_device(): lax.psum_scatter(jnp.einsum('kt,kfx->tfx', routing, compact, precision=la...  209 us
    another operation x1, loops' own time, on_device(): lax.fori_loop(0, live_slots[0], slot_step, jnp.zeros((slot_count, frame_c...  77.4 us
    slice x16, local copies, waits for them, and re-layouts, slot_step(): rf_rows[wave_index]  64.1 us
    psum x1, blocking collectives, on_device(): image_sum = lax.psum(owner_part[0], ('section', 'wave'))  32.4 us
    dynamic_slice x16, local copies, waits for them, and re-layouts, slot_step(): offsets[0, slot_index, wave_index] - history  21.9 us
    dot_general x16, matrix products, slot_step(): jnp.dot(filtered.reshape(wave_count * frame_count, tile_elems * window),...  21.3 us
    dynamic_slice x16, local copies, waits for them, and re-layouts, slot_step(): lax.dynamic_index_in_dim(apodization, fanout[0, slot_index], 1, keepdims=...  11.3 us
  transfers between devices with their start and end apart: 1, of which 1 were waited for; matrix products, arithmetic and copies ran while one was open for 0% of the time, Pallas kernels for 0%

commit v1 on v0

v1 whole, which is shorter than its diff:
```python
import functools

import jax
import jax.numpy as jnp
from jax import lax
from jax.experimental import pallas as pl
from jax.experimental.pallas import tpu as pltpu
from jax.sharding import PartitionSpec as P

LANES = 128


def beam_kernel(
    side, offsets, fanout, live, owned,
    rf, taps, weights, apod,
    keep, send,
    table, shifted, filtered, place,
):
    slot = pl.program_id(0)
    waves, frames, elems, samples = rf.shape
    window = weights.shape[1] // elems
    history = taps.shape[1]
    reach = window + history + LANES
    half = frames // 2
    tiles = owned.shape[0]

    @pl.when(slot == 0)
    def _():
        keep[...] = jnp.zeros_like(keep)
        send[...] = jnp.zeros_like(send)
        shifted[...] = jnp.zeros_like(shifted)
        rows = table.shape[0]
        line = jnp.concatenate(
            [
                jnp.zeros((1, window + history), jnp.float32),
                taps[...].astype(jnp.float32),
                jnp.zeros((1, rows - window - 2 * history), jnp.float32),
            ],
            axis=1,
        )
        spread = jnp.broadcast_to(line, (rows, rows))
        table[...] = pltpu.roll(spread, 0, 1, stride=1, stride_axis=0)[:, :window]

        def note(index, carry):
            place[owned[index]] = index
            return carry

        lax.fori_loop(0, tiles, note, 0)

    @pl.when(slot < live[0])
    def _():
        bases = []
        for wave in range(waves):
            start = offsets[0, slot, wave] - history
            base = jnp.minimum(start // LANES * LANES, samples - reach)
            shift = start - base
            shifted[
                wave * reach : (wave + 1) * reach, wave * window : (wave + 1) * window
            ] = table[pl.ds(LANES - shift, reach), :].astype(jnp.bfloat16)
            bases.append(pl.multiple_of(base, LANES))
        step = 16
        for first in range(0, frames, step):
            cut = jnp.concatenate(
                [
                    rf[wave, first : first + step, :, pl.ds(bases[wave], reach)].reshape(
                        step * elems, reach
                    )
                    for wave in range(waves)
                ],
                axis=1,
            )
            both = jnp.dot(cut, shifted[...], preferred_element_type=jnp.float32)
            for wave in range(waves):
                filtered[wave, first * elems : (first + step) * elems, :] = both[
                    :, wave * window : (wave + 1) * window
                ]
        beam = jnp.zeros((waves * frames, weights.shape[2]), jnp.float32)
        for elem in range(0, elems, 2):
            columns = []
            for each in (elem, elem + 1):
                columns.append(
                    jnp.concatenate(
                        [
                            filtered[w, pl.ds(each, frames, stride=elems), :].astype(jnp.bfloat16)
                            for w in range(waves)
                        ],
                        axis=0,
                    )
                )
            beam += jnp.dot(
                jnp.concatenate(columns, axis=1),
                weights[0, elem * window : (elem + 2) * window, :],
                preferred_element_type=jnp.float32,
            )
        voxel_tile = fanout[0, slot]
        term = jnp.zeros((frames, weights.shape[2]), jnp.float32)
        for wave in range(waves):
            term += apod[wave, pl.ds(voxel_tile, 1), :] * beam[wave * frames : (wave + 1) * frames]
        term -= jnp.sum(term, axis=0, keepdims=True) * (1.0 / frames)
        where = place[voxel_tile]
        swap = side[0] == 1
        keep[where] = jnp.where(swap, term[half:], term[:half])
        send[where] = jnp.where(swap, term[:half], term[half:])


def local_images(side, rf, taps, weights, apod, fanout, live, offsets, owned):
    waves, frames, elems, samples = rf.shape
    slots, depth, voxels = weights.shape[1:]
    window = depth // elems
    history = taps.shape[0]
    reach = window + history + LANES
    tiles = owned.shape[0]
    image = jax.ShapeDtypeStruct((tiles, frames // 2, voxels), jnp.float32)

    def whole(shape):
        return pl.BlockSpec(shape, lambda i, *_: (0,) * len(shape), pipeline_mode=pl.Buffered(1))

    return pl.pallas_call(
        beam_kernel,
        out_shape=(image, image),
        grid_spec=pltpu.PrefetchScalarGridSpec(
            num_scalar_prefetch=5,
            grid=(slots,),
            in_specs=[
                whole(rf.shape),
                whole((1, history)),
                pl.BlockSpec(
                    (None, 1, depth, voxels),
                    lambda i, side, offsets, fanout, live, owned: (
                        0, jnp.minimum(i, live[0] - 1), 0, 0,
                    ),
                ),
                whole(apod.shape),
            ],
            out_specs=[whole(image.shape), whole(image.shape)],
            scratch_shapes=[
                pltpu.VMEM((reach + LANES, window), jnp.float32),
                pltpu.VMEM((waves * reach, waves * window), jnp.bfloat16),
                pltpu.VMEM((waves, frames * elems, window), jnp.float32),
                pltpu.SMEM((tiles,), jnp.int32),
            ],
        ),
        compiler_params=pltpu.CompilerParams(
            dimension_semantics=("arbitrary",), vmem_limit_bytes=48 * 2**20
        ),
        name="beams",
    )(side, offsets, fanout, live, owned, rf, taps[None], weights, apod)


def on_device(
    rf_rows, filter_taps, interp_weights, apodization, fanout, live_slots, offsets, owned_tiles
):
    frames = rf_rows.shape[1]
    wave_groups = lax.axis_size("wave")
    side = lax.axis_index("section").astype(jnp.int32)[None]
    keep, send = local_images(
        side, rf_rows, filter_taps, interp_weights, apodization, fanout, live_slots, offsets,
        owned_tiles,
    )
    swap = [(0, 1), (1, 0)]
    pair = keep + lax.ppermute(send, "section", swap)
    parts = lax.all_to_all(pair, "tile", 0, 0, tiled=True)
    mine = jnp.sum(parts, axis=0)
    total = mine
    for hop in range(1, wave_groups):
        total = total + lax.ppermute(
            mine, "wave", [(i, (i + hop) % wave_groups) for i in range(wave_groups)]
        )
    power = jnp.sum(total * total, axis=0, keepdims=True) * (1.0 / frames)
    return power + lax.ppermute(power, "section", swap)


def solution(mesh):
    return jax.shard_map(
        on_device,
        mesh=mesh,
        in_specs=(
            P("wave", None, ("section", "tile"), None),
            P(),
            P(("section", "tile"), None, None, None),
            P("wave", None, None),
            P(("section", "tile"), None),
            P(("section", "tile")),
            P(("section", "tile"), None, "wave"),
            P(),
        ),
        out_specs=P("tile", None),
        check_vma=False,
    )
```

time: 489 us -> 67.2 us (0.14)
  waiting for transfers between devices: 209 us -> 5.88 us
  local copies, waits for them, and re-layouts: 123 us -> 3.48 us
  loops' own time: 77.4 us -> 0 us
  matrix products: 29.5 us -> 0 us
  Pallas kernels: 0 us -> 21.6 us
  between operations: 14.1 us -> 0.68 us
  starting transfers between devices: 0.01 us -> 8.54 us
  blocking collectives: 32.4 us -> 25.1 us
    reduce_scatter x1 -> x0, waiting for transfers between devices: 209 us -> none  [on_device(): lax.psum_scatter(jnp.einsum('kt,kfx->tfx', routing, compact, precision=la...]
    another operation x1 -> x0, loops' own time: 77.4 us -> none  [on_device(): lax.fori_loop(0, live_slots[0], slot_step, jnp.zeros((slot_count, frame_c...]
    slice x17 -> x0, local copies, waits for them, and re-layouts: 64.1 us -> none  [the longest x16 64.1 us: slot_step(): rf_rows[wave_index]]
    dynamic_slice x64 -> x0, local copies, waits for them, and re-layouts: 49.9 us -> none  [the longest x16 21.9 us: slot_step(): offsets[0, slot_index, wave_index] - history]
    psum x1 -> x0, blocking collectives: 32.4 us -> none  [on_device(): image_sum = lax.psum(owner_part[0], ('section', 'wave'))]
    dot_general x33 -> x0, matrix products: 29.5 us -> none  [the longest x16 21.3 us: slot_step(): jnp.dot(filtered.reshape(wave_count * frame_count, tile_elems * window),...]
    all_to_all x0 -> x1, blocking collectives: none -> 25.1 us  [on_device(): parts = lax.all_to_all(pair, 'tile', 0, 0, tiled=True)]
    pallas_call x0 -> x1, Pallas kernels: none -> 21.6 us  [local_images(): pl.pallas_call(beam_kernel, out_shape=(image, image), grid_spec=pltpu.Pre...]
  transfers between devices with their start and end apart: 1 -> 5, of which waited for: 1 -> 4; matrix products, arithmetic and copies ran while one was open for 0% -> 0% of each run, Pallas kernels for 0% -> 0%
where the time goes in v1:
time: 67.2 us; the launch traced here: 66 us
  blocking collectives  25.1 us (37%)
  Pallas kernels  21.6 us (32%)
  starting transfers between devices  8.54 us (13%)
  waiting for transfers between devices  5.88 us (9%)
  local copies, waits for them, and re-layouts  3.48 us (5%)
  between operations  0.68 us (1%)
    all_to_all x1, blocking collectives, on_device(): parts = lax.all_to_all(pair, 'tile', 0, 0, tiled=True)  25.1 us
    pallas_call x1, Pallas kernels, local_images(): pl.pallas_call(beam_kernel, out_shape=(image, image), grid_spec=pltpu.Pre...  21.6 us
    ppermute x1, starting transfers between devices, on_device(): return power + lax.ppermute(power, 'section', swap)  4.69 us
    ppermute x3, starting transfers between devices, on_device(): lax.ppermute(mine, 'wave', [(i, (i + hop) % wave_groups) for i in range(w...  3.76 us
    unnamed x9, local copies, waits for them, and re-layouts  3.48 us
    ppermute x3, waiting for transfers between devices, on_device(): lax.ppermute(mine, 'wave', [(i, (i + hop) % wave_groups) for i in range(w...  3.16 us
    ppermute x1, waiting for transfers between devices, on_device(): pair = keep + lax.ppermute(send, 'section', swap)  1.9 us
  transfers between devices with their start and end apart: 5, of which 4 were waited for; matrix products, arithmetic and copies ran while one was open for 0% of the time, Pallas kernels for 0%

profile of v1, /device:TPU:1, one launch (start us, length us, event | category | flops | bytes accessed | tf_op | source)
XLA Modules:
  0.0 66.0 jit_solution(11480982290203362672)
XLA Ops:
  0.7 0.8 %copy.10.offsets = s32[1,16,2]{2,1,0:T(8,128)S(1)} copy(s32[1,16,2]{1,2,0:T(2,128)} %param.14) | data formatting | bytes 256 | tf_op args[6]
  1.4 0.0 copy-start
  1.4 0.8 %copy-done = f32[2,32,128]{2,1,0:T(8,128)S(1)} copy-done((f32[2,32,128]{2,1,0:T(8,128)S(1)}, f32[2,32,128]{2,1,0:T(8,128)}, u32[]{:S(2)}) %copy-start) | copy-done | bytes 32792
  2.2 0.0 copy-start.1
  2.2 0.7 copy-done.1
  2.8 0.0 copy-start.2
  2.8 0.7 copy-done.2
  3.5 0.0 copy-start.3
  3.5 0.7 copy-done.3
  4.1 21.6 %beams.1 = (f32[32,32,128]{2,1,0:T(8,128)S(1)}, f32[32,32,128]{2,1,0:T(8,128)S(1)}) custom-call(s32[1]{0:T(128)} %bitcast.side, s32[1,16,2]{2,1,0:T(8,128)S(1)} %copy.10.offsets, s32[1,16]{1,0:T(1,128)S(1)} %copy-done.1, s32[1]{0:T(128)S(6)} %copy.11.live, s32[32]{0:T(128)S(1)} %copy-done.2, bf16[2,64,16,2048]{3,2,1,0:T(8,128)(2,1)} %rf.1, ...), custom_call_target="tpu_custom_call" | custom-call | tf_op jit(solution)/shard_map/beams/pallas_call | solution.py:118
  25.8 0.1 collective-permute-start
  25.9 1.9 %collective-permute-done = f32[32,32,128]{2,1,0:T(8,128)S(1)} collective-permute-done((f32[32,32,128]{2,1,0:T(8,128)S(1)}, f32[32,32,128]{2,1,0:T(8,128)S(1)}, u32[]{:S(2)}, u32[]{:S(2)}) %collective-permute-start) | collective-permute-done | bytes 524320 | tf_op jit(solution)/shard_map/ppermute | solution.py:161
  27.8 0.1 add.15
  27.9 25.1 %all_to_all.5 = f32[32,32,128]{2,1,0:T(8,128)S(1)} all-to-all(f32[32,32,128]{2,1,0:T(8,128)S(1)} %add.15), channel_id=1, replica_groups=mesh['section'=2,'tile'=32,'wave'=4] {'tile'}, dimensions={0} | all-to-all | bytes 1048576 | tf_op jit(solution)/shard_map/all_to_all | solution.py:162
  53.0 2.4 %collective-permute-start.3 = (f32[32,128]{1,0:T(8,128)S(1)}, f32[32,128]{1,0:T(8,128)S(1)}, u32[]{:S(2)}, u32[]{:S(2)}) collective-permute-start(f32[32,128]{1,0:T(8,128)S(1)} %reduce_sum.18), channel_id=1, source_target_pairs={{0,3},{1,0},{2,1},{3,2},{4,7},{5,4},{6,5},{7,6},{8,11},{9,8},{10,9... | collective-permute-start | bytes 49160 | tf_op jit(solution)/shard_map/ppermute | solution.py:166
  55.4 0.7 %collective-permute-start.2 = (f32[32,128]{1,0:T(8,128)S(1)}, f32[32,128]{1,0:T(8,128)S(1)}, u32[]{:S(2)}, u32[]{:S(2)}) collective-permute-start(f32[32,128]{1,0:T(8,128)S(1)} %reduce_sum.18), channel_id=1, source_target_pairs={{0,2},{1,3},{2,0},{3,1},{4,6},{5,7},{6,4},{7,5},{8,10},{9,11},{10,... | collective-permute-start | bytes 49160 | tf_op jit(solution)/shard_map/ppermute | solution.py:166
  56.2 0.6 collective-permute-start.1
  56.8 0.0 collective-permute-done.3
  56.8 2.7 %collective-permute-done.2 = f32[32,128]{1,0:T(8,128)S(1)} collective-permute-done((f32[32,128]{1,0:T(8,128)S(1)}, f32[32,128]{1,0:T(8,128)S(1)}, u32[]{:S(2)}, u32[]{:S(2)}) %collective-permute-start.2) | collective-permute-done | bytes 16416 | tf_op jit(solution)/shard_map/ppermute | solution.py:166
  59.5 0.4 collective-permute-done.1
  60.0 4.7 %collective-permute-start.4 = (f32[1,128]{1,0:T(1,128)S(1)}, f32[1,128]{1,0:T(1,128)S(1)}, u32[]{:S(2)}, u32[]{:S(2)}) collective-permute-start(f32[1,128]{1,0:T(1,128)S(1)} %multiply_bitcast_fusion), channel_id=1, source_target_pairs={{0,128},{128,0},{1,129},{129,1},{2,130},{130,2},{3,131},{131,3},{4... | collective-permute-start | bytes 1544 | tf_op jit(solution)/shard_map/ppermute | solution.py:170
  64.7 0.8 %collective-permute-done.4 = f32[1,128]{1,0:T(1,128)S(1)} collective-permute-done((f32[1,128]{1,0:T(1,128)S(1)}, f32[1,128]{1,0:T(1,128)S(1)}, u32[]{:S(2)}, u32[]{:S(2)}) %collective-permute-start.4) | collective-permute-done | bytes 544 | tf_op jit(solution)/shard_map/ppermute | solution.py:170
  65.5 0.5 fusion
  (3 shorter events, 0.1 us)
Async XLA Ops:
  1.4 0.8 %copy-start = (f32[2,32,128]{2,1,0:T(8,128)S(1)}, f32[2,32,128]{2,1,0:T(8,128)}, u32[]{:S(2)}) copy-start(f32[2,32,128]{2,1,0:T(8,128)} %apod.1) | copy-start | bytes 98308
  2.2 0.7 copy-start.1
  2.8 0.7 copy-start.2
  3.5 0.7 copy-start.3
  25.8 2.0 %collective-permute-start = (f32[32,32,128]{2,1,0:T(8,128)S(1)}, f32[32,32,128]{2,1,0:T(8,128)S(1)}, u32[]{:S(2)}, u32[]{:S(2)}) collective-permute-start(f32[32,32,128]{2,1,0:T(8,128)S(1)} %get-tuple-element.8), channel_id=1, source_target_pairs={{0,128},{128,0},{1,129},{129,1},{2,130},{130,2},{3,131},{131,3},{4... | collective-permute-start | bytes 1572872 | tf_op jit(solution)/shard_map/ppermute | solution.py:161
  53.0 3.8 %collective-permute-start.3 = (f32[32,128]{1,0:T(8,128)S(1)}, f32[32,128]{1,0:T(8,128)S(1)}, u32[]{:S(2)}, u32[]{:S(2)}) collective-permute-start(f32[32,128]{1,0:T(8,128)S(1)} %reduce_sum.18), channel_id=1, source_target_pairs={{0,3},{1,0},{2,1},{3,2},{4,7},{5,4},{6,5},{7,6},{8,11},{9,8},{10,9... | collective-permute-start | bytes 49160 | tf_op jit(solution)/shard_map/ppermute | solution.py:166
  55.4 4.1 %collective-permute-start.2 = (f32[32,128]{1,0:T(8,128)S(1)}, f32[32,128]{1,0:T(8,128)S(1)}, u32[]{:S(2)}, u32[]{:S(2)}) collective-permute-start(f32[32,128]{1,0:T(8,128)S(1)} %reduce_sum.18), channel_id=1, source_target_pairs={{0,2},{1,3},{2,0},{3,1},{4,6},{5,7},{6,4},{7,5},{8,10},{9,11},{10,... | collective-permute-start | bytes 49160 | tf_op jit(solution)/shard_map/ppermute | solution.py:166
  56.2 3.8 %collective-permute-start.1 = (f32[32,128]{1,0:T(8,128)S(1)}, f32[32,128]{1,0:T(8,128)S(1)}, u32[]{:S(2)}, u32[]{:S(2)}) collective-permute-start(f32[32,128]{1,0:T(8,128)S(1)} %reduce_sum.18), channel_id=1, source_target_pairs={{0,1},{1,2},{2,3},{3,0},{4,5},{5,6},{6,7},{7,4},{8,9},{9,10},{10,1... | collective-permute-start | bytes 49160 | tf_op jit(solution)/shard_map/ppermute | solution.py:166
  60.0 5.5 %collective-permute-start.4 = (f32[1,128]{1,0:T(1,128)S(1)}, f32[1,128]{1,0:T(1,128)S(1)}, u32[]{:S(2)}, u32[]{:S(2)}) collective-permute-start(f32[1,128]{1,0:T(1,128)S(1)} %multiply_bitcast_fusion), channel_id=1, source_target_pairs={{0,128},{128,0},{1,129},{129,1},{2,130},{130,2},{3,131},{131,3},{4... | collective-permute-start | bytes 1544 | tf_op jit(solution)/shard_map/ppermute | solution.py:170

commit v2 on v1

v2 whole, which is shorter than its diff:
```python
import jax
import jax.numpy as jnp
from jax import lax
from jax.experimental import pallas as pl
from jax.experimental.pallas import tpu as pltpu
from jax.sharding import PartitionSpec as P

LANES = 128
SUBLANES = 8
STEP = 16


def beam_kernel(
    side, live, offsets_in, fanout_in, owned_in, rf_in, taps_in, weights_in, apod_in,
    keep, send,
    offsets, fanout, owned, place, taps, apod, rf, weights,
    table, shifted, filtered, other, small_sems, rf_sems, weight_sems,
):
    waves, frames, elems, samples = rf.shape
    slots, depth, voxels = weights.shape
    window = depth // elems
    history = taps.shape[1]
    reach = window + history + LANES
    half = frames // 2
    tiles = owned.shape[0]
    chunks = frames // STEP
    small = [
        pltpu.make_async_copy(source, target, small_sems.at[i])
        for i, (source, target) in enumerate(
            [
                (offsets_in, offsets), (fanout_in, fanout), (owned_in, owned),
                (taps_in, taps), (apod_in, apod),
            ]
        )
    ]

    def rf_copy(chunk):
        span = pl.ds(chunk * STEP, STEP)
        return pltpu.make_async_copy(rf_in.at[:, span], rf.at[:, span], rf_sems.at[chunk])

    def weight_copy(slot):
        return pltpu.make_async_copy(weights_in.at[0, slot], weights.at[slot], weight_sems.at[slot])

    for copy in small:
        copy.start()
    for chunk in range(chunks):
        rf_copy(chunk).start()
    count = live[0]
    pairs = (count + 1) // 2
    keep[...] = jnp.zeros_like(keep)
    send[...] = jnp.zeros_like(send)
    for copy in small:
        copy.wait()
    for slot in range(slots):

        @pl.when(slot < 2 * pairs)
        def _():
            weight_copy(slot).start()

    rows = reach + LANES
    line = jnp.concatenate(
        [
            jnp.zeros((1, window + history), jnp.float32),
            taps[...].astype(jnp.float32),
            jnp.zeros((1, rows - window - 2 * history), jnp.float32),
        ],
        axis=1,
    )
    spread = jnp.broadcast_to(line, (rows, rows))
    table[...] = pltpu.roll(spread, 0, 1, stride=1, stride_axis=0)[:, :window]

    def note(index, carry):
        place[owned[index]] = index
        return carry

    lax.fori_loop(0, tiles, note, 0)

    def aim(slot, turn):
        bases = []
        for wave in range(waves):
            start = offsets[0, wave, slot] - history
            base = jnp.minimum(start // LANES * LANES, samples - reach)
            shifted[turn, wave] = table[pl.ds(LANES - (start - base), reach), :].astype(
                jnp.bfloat16
            )
            bases.append(pl.multiple_of(base, LANES))
        return bases

    def fir(bases, first, target, turn):
        for wave in range(waves):
            cut = rf[wave, first : first + STEP, :, pl.ds(bases[wave], reach)].reshape(
                STEP * elems, reach
            )
            lines = jnp.dot(cut, shifted[turn, wave], preferred_element_type=jnp.float32).reshape(
                STEP, elems // SUBLANES, SUBLANES, window
            )
            for part in range(elems // SUBLANES):
                target[wave, part, first * SUBLANES : (first + STEP) * SUBLANES, :] = lines[
                    :, part
                ].reshape(STEP * SUBLANES, window)

    def interpolate(slot, elem, source):
        columns = []
        for each in (elem, elem + 1):
            lines = [
                source[
                    wave, each // SUBLANES, pl.ds(each % SUBLANES, frames, stride=SUBLANES), :
                ].astype(jnp.bfloat16)
                for wave in range(waves)
            ]
            columns.append(jnp.concatenate(lines, axis=0))
        return jnp.dot(
            jnp.concatenate(columns, axis=1),
            weights[slot, elem * window : (elem + 2) * window, :],
            preferred_element_type=jnp.float32,
        )

    def finish(slot, beam):
        voxel_tile = fanout[0, slot]
        term = jnp.zeros((frames, voxels), jnp.float32)
        for wave in range(waves):
            term += apod[wave, pl.ds(voxel_tile, 1), :] * beam[wave * frames : (wave + 1) * frames]
        term -= jnp.sum(term, axis=0, keepdims=True) * (1.0 / frames)
        where = place[voxel_tile]
        alive = slot < count
        swap = side[0] == 1
        keep[where] = jnp.where(alive, jnp.where(swap, term[half:], term[:half]), keep[where])
        send[where] = jnp.where(alive, jnp.where(swap, term[:half], term[half:]), send[where])

    def stage(slot, source, target, turn):
        bases = aim(jnp.minimum(slot + 1, slots - 1), turn)
        beam = jnp.zeros((waves * frames, voxels), jnp.float32)
        total = elems // 2
        done = 0
        for chunk in range(chunks):
            fir(bases, chunk * STEP, target, turn)
            goal = min(total, -(-total * (chunk + 1) // (chunks - 1)))
            for pair in range(done, goal):
                beam += interpolate(slot, pair * 2, source)
            if done < total and goal == total:
                finish(slot, beam)
            done = goal

    bases = aim(0, 1)
    for chunk in range(chunks):
        rf_copy(chunk).wait()
        fir(bases, chunk * STEP, filtered, 1)

    def two_slots(index, carry):
        weight_copy(2 * index).wait()
        weight_copy(2 * index + 1).wait()
        stage(2 * index, filtered, other, 0)
        stage(2 * index + 1, other, filtered, 1)
        return carry

    lax.fori_loop(0, pairs, two_slots, 0)


def local_images(side, rf, taps, weights, apod, fanout, live, offsets, owned, opts=()):
    waves, frames, elems, samples = rf.shape
    slots, depth, voxels = weights.shape[1:]
    window = depth // elems
    history = taps.shape[0]
    reach = window + history + LANES
    tiles = owned.shape[0]
    image = jax.ShapeDtypeStruct((tiles, frames // 2, voxels), jnp.float32)
    smem = pl.BlockSpec(memory_space=pltpu.SMEM)
    hbm = pl.BlockSpec(memory_space=pltpu.HBM)
    vmem = pl.BlockSpec(memory_space=pltpu.VMEM)
    lines = pltpu.VMEM((waves, elems // SUBLANES, frames * SUBLANES, window), jnp.float32)
    return pl.pallas_call(
        beam_kernel,
        out_shape=(image, image),
        in_specs=[smem, smem] + [hbm] * 7,
        out_specs=[vmem, vmem],
        scratch_shapes=[
            pltpu.SMEM((1, waves, slots), jnp.int32),
            pltpu.SMEM((1, slots), jnp.int32),
            pltpu.SMEM((tiles,), jnp.int32),
            pltpu.SMEM((tiles,), jnp.int32),
            pltpu.VMEM((1, history), jnp.bfloat16),
            pltpu.VMEM(apod.shape, jnp.float32),
            pltpu.VMEM(rf.shape, jnp.bfloat16),
            pltpu.VMEM(weights.shape[1:], jnp.bfloat16),
            pltpu.VMEM((reach + LANES, window), jnp.float32),
            pltpu.VMEM((2, waves, reach, window), jnp.bfloat16),
            lines,
            lines,
            pltpu.SemaphoreType.DMA((5,)),
            pltpu.SemaphoreType.DMA((frames // STEP,)),
            pltpu.SemaphoreType.DMA((slots,)),
        ],
        compiler_params=pltpu.CompilerParams(vmem_limit_bytes=48 * 2**20),
        name="beams",
    )(
        side,
        live,
        *[
            pltpu.with_memory_space_constraint(array, pltpu.HBM)
            for array in (
                offsets.transpose(0, 2, 1), fanout, owned, rf, taps[None], weights, apod,
            )
        ],
    )


def on_device(
    rf_rows, filter_taps, interp_weights, apodization, fanout, live_slots, offsets, owned_tiles
):
    frames = rf_rows.shape[1]
    wave_groups = lax.axis_size("wave")
    side = lax.axis_index("section").astype(jnp.int32)[None]
    keep, send = local_images(
        side, rf_rows, filter_taps, interp_weights, apodization, fanout, live_slots, offsets,
        owned_tiles,
    )
    swap = [(0, 1), (1, 0)]
    pair = keep + lax.ppermute(send, "section", swap)
    parts = lax.all_to_all(pair, "tile", 0, 0, tiled=True)
    mine = jnp.sum(parts, axis=0)
    total = mine
    for hop in range(1, wave_groups):
        total = total + lax.ppermute(
            mine, "wave", [(i, (i + hop) % wave_groups) for i in range(wave_groups)]
        )
    power = jnp.sum(total * total, axis=0, keepdims=True) * (1.0 / frames)
    return power + lax.ppermute(power, "section", swap)


def solution(mesh):
    return jax.shard_map(
        on_device,
        mesh=mesh,
        in_specs=(
            P("wave", None, ("section", "tile"), None),
            P(),
            P(("section", "tile"), None, None, None),
            P("wave", None, None),
            P(("section", "tile"), None),
            P(("section", "tile")),
            P(("section", "tile"), None, "wave"),
            P(),
        ),
        out_specs=P("tile", None),
        check_vma=False,
    )
```

time: 67.2 us -> 57.4 us (0.85)
  Pallas kernels: 21.6 us -> 8.18 us
  starting transfers between devices: 8.54 us -> 16.7 us
  local copies, waits for them, and re-layouts: 3.48 us -> 0 us
    pallas_call x1, Pallas kernels: 21.6 us -> 8.18 us  [local_images(): pl.pallas_call(beam_kernel, out_shape=(image, image), in_specs=[smem, sme...]
    ppermute x1, starting transfers between devices: 0.09 us -> 7.56 us  [on_device(): pair = keep + lax.ppermute(send, 'section', swap)]
    unnamed x9 -> x0, local copies, waits for them, and re-layouts: 3.48 us -> none
where the time goes in v2:
time: 57.4 us; the launch traced here: 56.7 us
  blocking collectives  25 us (44%)
  starting transfers between devices  16.7 us (29%)
  Pallas kernels  8.18 us (14%)
  waiting for transfers between devices  5.5 us (10%)
  other arithmetic  0.67 us (1%)
  between operations  0.67 us (1%)
    all_to_all x1, blocking collectives, on_device(): parts = lax.all_to_all(pair, 'tile', 0, 0, tiled=True)  25 us
    pallas_call x1, Pallas kernels, local_images(): pl.pallas_call(beam_kernel, out_shape=(image, image), in_specs=[smem, sme...  8.18 us
    ppermute x1, starting transfers between devices, on_device(): pair = keep + lax.ppermute(send, 'section', swap)  7.56 us
    ppermute x1, starting transfers between devices, on_device(): return power + lax.ppermute(power, 'section', swap)  5.32 us
    ppermute x3, starting transfers between devices, on_device(): lax.ppermute(mine, 'wave', [(i, (i + hop) % wave_groups) for i in range(w...  3.79 us
    ppermute x3, waiting for transfers between devices, on_device(): lax.ppermute(mine, 'wave', [(i, (i + hop) % wave_groups) for i in range(w...  3.15 us
    ppermute x1, waiting for transfers between devices, on_device(): pair = keep + lax.ppermute(send, 'section', swap)  1.54 us
  transfers between devices with their start and end apart: 5, of which 4 were waited for; matrix products, arithmetic and copies ran while one was open for 0% of the time, Pallas kernels for 0%

profile of v2, /device:TPU:1, one launch (start us, length us, event | category | flops | bytes accessed | tf_op | source)
XLA Modules:
  0.0 56.7 jit_solution(14018584969526705043)
XLA Ops:
  0.7 8.2 %beams.1 = (f32[32,32,128]{2,1,0:T(8,128)S(1)}, f32[32,32,128]{2,1,0:T(8,128)S(1)}) custom-call(s32[1]{0:T(128)} %bitcast.side, s32[1]{0:T(128)S(6)} %copy.9.live, s32[1,2,16]{2,1,0:T(2,128)} %bitcast.7, s32[1,16]{1,0:T(1,128)} %fanout_in.1, s32[32]{0:T(128)} %owned_in.1, bf16[2,64,16,2048]{3,2,1,0:T(8,128)(2,1)} %rf_in.1, bf16[1,128]{1,0:T(2,128)(2,1)} %bitcast.8, ...), custom_call_target="tpu_custom_call" | custom-call | tf_op jit(solution)/shard_map/beams/pallas_call | solution.py:171
  8.8 7.6 %collective-permute-start = (f32[32,32,128]{2,1,0:T(8,128)S(1)}, f32[32,32,128]{2,1,0:T(8,128)S(1)}, u32[]{:S(2)}, u32[]{:S(2)}) collective-permute-start(f32[32,32,128]{2,1,0:T(8,128)S(1)} %get-tuple-element.8), channel_id=1, source_target_pairs={{0,128},{128,0},{1,129},{129,1},{2,130},{130,2},{3,131},{131,3},{4... | collective-permute-start | bytes 1572872 | tf_op jit(solution)/shard_map/ppermute | solution.py:218
  16.4 1.5 %collective-permute-done = f32[32,32,128]{2,1,0:T(8,128)S(1)} collective-permute-done((f32[32,32,128]{2,1,0:T(8,128)S(1)}, f32[32,32,128]{2,1,0:T(8,128)S(1)}, u32[]{:S(2)}, u32[]{:S(2)}) %collective-permute-start) | collective-permute-done | bytes 524320 | tf_op jit(solution)/shard_map/ppermute | solution.py:218
  17.9 0.1 add.15
  18.0 25.0 %all_to_all.5 = f32[32,32,128]{2,1,0:T(8,128)S(1)} all-to-all(f32[32,32,128]{2,1,0:T(8,128)S(1)} %add.15), channel_id=1, replica_groups=mesh['section'=2,'tile'=32,'wave'=4] {'tile'}, dimensions={0} | all-to-all | bytes 1048576 | tf_op jit(solution)/shard_map/all_to_all | solution.py:219
  43.0 2.7 %collective-permute-start.3 = (f32[32,128]{1,0:T(8,128)S(1)}, f32[32,128]{1,0:T(8,128)S(1)}, u32[]{:S(2)}, u32[]{:S(2)}) collective-permute-start(f32[32,128]{1,0:T(8,128)S(1)} %reduce_sum.18), channel_id=1, source_target_pairs={{0,3},{1,0},{2,1},{3,2},{4,7},{5,4},{6,5},{7,6},{8,11},{9,8},{10,9... | collective-permute-start | bytes 49160 | tf_op jit(solution)/shard_map/ppermute | solution.py:223
  45.7 0.5 collective-permute-start.2
  46.2 0.7 %collective-permute-start.1 = (f32[32,128]{1,0:T(8,128)S(1)}, f32[32,128]{1,0:T(8,128)S(1)}, u32[]{:S(2)}, u32[]{:S(2)}) collective-permute-start(f32[32,128]{1,0:T(8,128)S(1)} %reduce_sum.18), channel_id=1, source_target_pairs={{0,1},{1,2},{2,3},{3,0},{4,5},{5,6},{6,7},{7,4},{8,9},{9,10},{10,1... | collective-permute-start | bytes 49160 | tf_op jit(solution)/shard_map/ppermute | solution.py:223
  46.8 0.0 collective-permute-done.3
  46.8 3.0 %collective-permute-done.2 = f32[32,128]{1,0:T(8,128)S(1)} collective-permute-done((f32[32,128]{1,0:T(8,128)S(1)}, f32[32,128]{1,0:T(8,128)S(1)}, u32[]{:S(2)}, u32[]{:S(2)}) %collective-permute-start.2) | collective-permute-done | bytes 16416 | tf_op jit(solution)/shard_map/ppermute | solution.py:223
  49.8 0.2 collective-permute-done.1
  50.0 5.3 %collective-permute-start.4 = (f32[1,128]{1,0:T(1,128)S(1)}, f32[1,128]{1,0:T(1,128)S(1)}, u32[]{:S(2)}, u32[]{:S(2)}) collective-permute-start(f32[1,128]{1,0:T(1,128)S(1)} %multiply_bitcast_fusion), channel_id=1, source_target_pairs={{0,128},{128,0},{1,129},{129,1},{2,130},{130,2},{3,131},{131,3},{4... | collective-permute-start | bytes 1544 | tf_op jit(solution)/shard_map/ppermute | solution.py:227
  55.3 0.8 %collective-permute-done.4 = f32[1,128]{1,0:T(1,128)S(1)} collective-permute-done((f32[1,128]{1,0:T(1,128)S(1)}, f32[1,128]{1,0:T(1,128)S(1)}, u32[]{:S(2)}, u32[]{:S(2)}) %collective-permute-start.4) | collective-permute-done | bytes 544 | tf_op jit(solution)/shard_map/ppermute | solution.py:227
  56.2 0.5 fusion
  (3 shorter events, 0.1 us)
Async XLA Ops:
  8.8 9.1 %collective-permute-start = (f32[32,32,128]{2,1,0:T(8,128)S(1)}, f32[32,32,128]{2,1,0:T(8,128)S(1)}, u32[]{:S(2)}, u32[]{:S(2)}) collective-permute-start(f32[32,32,128]{2,1,0:T(8,128)S(1)} %get-tuple-element.8), channel_id=1, source_target_pairs={{0,128},{128,0},{1,129},{129,1},{2,130},{130,2},{3,131},{131,3},{4... | collective-permute-start | bytes 1572872 | tf_op jit(solution)/shard_map/ppermute | solution.py:218
  43.0 3.8 %collective-permute-start.3 = (f32[32,128]{1,0:T(8,128)S(1)}, f32[32,128]{1,0:T(8,128)S(1)}, u32[]{:S(2)}, u32[]{:S(2)}) collective-permute-start(f32[32,128]{1,0:T(8,128)S(1)} %reduce_sum.18), channel_id=1, source_target_pairs={{0,3},{1,0},{2,1},{3,2},{4,7},{5,4},{6,5},{7,6},{8,11},{9,8},{10,9... | collective-permute-start | bytes 49160 | tf_op jit(solution)/shard_map/ppermute | solution.py:223
  45.7 4.1 %collective-permute-start.2 = (f32[32,128]{1,0:T(8,128)S(1)}, f32[32,128]{1,0:T(8,128)S(1)}, u32[]{:S(2)}, u32[]{:S(2)}) collective-permute-start(f32[32,128]{1,0:T(8,128)S(1)} %reduce_sum.18), channel_id=1, source_target_pairs={{0,2},{1,3},{2,0},{3,1},{4,6},{5,7},{6,4},{7,5},{8,10},{9,11},{10,... | collective-permute-start | bytes 49160 | tf_op jit(solution)/shard_map/ppermute | solution.py:223
  46.2 3.8 %collective-permute-start.1 = (f32[32,128]{1,0:T(8,128)S(1)}, f32[32,128]{1,0:T(8,128)S(1)}, u32[]{:S(2)}, u32[]{:S(2)}) collective-permute-start(f32[32,128]{1,0:T(8,128)S(1)} %reduce_sum.18), channel_id=1, source_target_pairs={{0,1},{1,2},{2,3},{3,0},{4,5},{5,6},{6,7},{7,4},{8,9},{9,10},{10,1... | collective-permute-start | bytes 49160 | tf_op jit(solution)/shard_map/ppermute | solution.py:223
  50.0 6.1 %collective-permute-start.4 = (f32[1,128]{1,0:T(1,128)S(1)}, f32[1,128]{1,0:T(1,128)S(1)}, u32[]{:S(2)}, u32[]{:S(2)}) collective-permute-start(f32[1,128]{1,0:T(1,128)S(1)} %multiply_bitcast_fusion), channel_id=1, source_target_pairs={{0,128},{128,0},{1,129},{129,1},{2,130},{130,2},{3,131},{131,3},{4... | collective-permute-start | bytes 1544 | tf_op jit(solution)/shard_map/ppermute | solution.py:227

commit v3 on v2

--- a/solution.py
+++ b/solution.py
@@ -8,10 +8,11 @@
 LANES = 128
 SUBLANES = 8
 STEP = 16
+ROWS = 4
 
 
 def beam_kernel(
-    side, live, offsets_in, fanout_in, owned_in, rf_in, taps_in, weights_in, apod_in,
+    side, row, live, offsets_in, fanout_in, owned_in, rf_in, taps_in, weights_in, apod_in,
     keep, send,
     offsets, fanout, owned, place, taps, apod, rf, weights,
     table, shifted, filtered, other, small_sems, rf_sems, weight_sems,
@@ -69,8 +70,11 @@
     spread = jnp.broadcast_to(line, (rows, rows))
     table[...] = pltpu.roll(spread, 0, 1, stride=1, stride_axis=0)[:, :window]
 
+    columns = tiles // ROWS
+
     def note(index, carry):
-        place[owned[index]] = index
+        ahead = lax.rem(index // columns - row[0] + ROWS, ROWS)
+        place[owned[index]] = ahead * columns + lax.rem(index, columns)
         return carry
 
     lax.fori_loop(0, tiles, note, 0)
@@ -156,7 +160,7 @@
     lax.fori_loop(0, pairs, two_slots, 0)
 
 
-def local_images(side, rf, taps, weights, apod, fanout, live, offsets, owned, opts=()):
+def local_images(side, row, rf, taps, weights, apod, fanout, live, offsets, owned, opts=()):
     waves, frames, elems, samples = rf.shape
     slots, depth, voxels = weights.shape[1:]
     window = depth // elems
@@ -171,7 +175,7 @@
     return pl.pallas_call(
         beam_kernel,
         out_shape=(image, image),
-        in_specs=[smem, smem] + [hbm] * 7,
+        in_specs=[smem, smem, smem] + [hbm] * 7,
         out_specs=[vmem, vmem],
         scratch_shapes=[
             pltpu.SMEM((1, waves, slots), jnp.int32),
@@ -194,6 +198,7 @@
         name="beams",
     )(
         side,
+        row,
         live,
         *[
             pltpu.with_memory_space_constraint(array, pltpu.HBM)
@@ -209,14 +214,27 @@
 ):
     frames = rf_rows.shape[1]
     wave_groups = lax.axis_size("wave")
+    tiles = lax.axis_size("tile")
+    columns = tiles // ROWS
     side = lax.axis_index("section").astype(jnp.int32)[None]
+    row = lax.div(lax.axis_index("tile").astype(jnp.int32), jnp.int32(columns))[None]
     keep, send = local_images(
-        side, rf_rows, filter_taps, interp_weights, apodization, fanout, live_slots, offsets,
+        side, row, rf_rows, filter_taps, interp_weights, apodization, fanout, live_slots, offsets,
         owned_tiles,
     )
     swap = [(0, 1), (1, 0)]
-    pair = keep + lax.ppermute(send, "section", swap)
-    parts = lax.all_to_all(pair, "tile", 0, 0, tiled=True)
+    got = lax.ppermute(send, "section", swap)
+    pairs = [
+        keep[at * columns : (at + 1) * columns] + got[at * columns : (at + 1) * columns]
+        for at in range(ROWS)
+    ]
+    line = pairs[0]
+    for hop in range(1, ROWS):
+        line = line + lax.ppermute(
+            pairs[hop], "tile", [(i, (i + hop * columns) % tiles) for i in range(tiles)]
+        )
+    groups = [[at * columns + i for i in range(columns)] for at in range(ROWS)]
+    parts = lax.all_to_all(line, "tile", 0, 0, axis_index_groups=groups, tiled=True)
     mine = jnp.sum(parts, axis=0)
     total = mine
     for hop in range(1, wave_groups):

time: 57.4 us -> 57.8 us (level)
  waiting for transfers between devices: 5.5 us -> 10.8 us
  blocking collectives: 25 us -> 20.3 us
  starting transfers between devices: 16.7 us -> 18.3 us
  Pallas kernels: 8.18 us -> 6.8 us
    ppermute x1 -> x4, waiting for transfers between devices: 1.54 us -> 6.86 us  [the longest x3 5.32 us: on_device(): lax.ppermute(pairs[hop], 'tile', [(i, (i + hop * columns) % tiles) for i...]
    all_to_all x1, blocking collectives: 25 us -> 20.3 us  [on_device(): lax.all_to_all(line, 'tile', 0, 0, axis_index_groups=groups, tiled=True)]
    ppermute x1 -> x4, starting transfers between devices: 7.56 us -> 10.3 us  [the longest x1 7.55 us: on_device(): got = lax.ppermute(send, 'section', swap)]
    pallas_call x1, Pallas kernels: 8.18 us -> 6.8 us  [local_images(): pl.pallas_call(beam_kernel, out_shape=(image, image), in_specs=[smem, sme...]
    ppermute x1, starting transfers between devices: 5.32 us -> 4.32 us  [on_device(): return power + lax.ppermute(power, 'section', swap)]
  transfers between devices with their start and end apart: 5 -> 8, of which waited for: 4 -> 7; matrix products, arithmetic and copies ran while one was open for 0% -> 0% of each run, Pallas kernels for 0% -> 0%
where the time goes in v3:
time: 57.8 us; the launch traced here: 57.6 us
  blocking collectives  20.3 us (35%)
  starting transfers between devices  18.3 us (32%)
  waiting for transfers between devices  10.8 us (19%)
  Pallas kernels  6.8 us (12%)
  between operations  0.68 us (1%)
  other arithmetic  0.67 us (1%)
    all_to_all x1, blocking collectives, on_device(): lax.all_to_all(line, 'tile', 0, 0, axis_index_groups=groups, tiled=True)  20.3 us
    ppermute x1, starting transfers between devices, on_device(): got = lax.ppermute(send, 'section', swap)  7.55 us
    pallas_call x1, Pallas kernels, local_images(): pl.pallas_call(beam_kernel, out_shape=(image, image), in_specs=[smem, sme...  6.8 us
    ppermute x3, waiting for transfers between devices, on_device(): lax.ppermute(pairs[hop], 'tile', [(i, (i + hop * columns) % tiles) for i...  5.32 us
    ppermute x1, starting transfers between devices, on_device(): return power + lax.ppermute(power, 'section', swap)  4.32 us
    ppermute x3, starting transfers between devices, on_device(): lax.ppermute(mine, 'wave', [(i, (i + hop) % wave_groups) for i in range(w...  3.7 us
    ppermute x3, waiting for transfers between devices, on_device(): lax.ppermute(mine, 'wave', [(i, (i + hop) % wave_groups) for i in range(w...  3.13 us
    ppermute x3, starting transfers between devices, on_device(): lax.ppermute(pairs[hop], 'tile', [(i, (i + hop * columns) % tiles) for i...  2.75 us
  transfers between devices with their start and end apart: 8, of which 7 were waited for; matrix products, arithmetic and copies ran while one was open for 0% of the time, Pallas kernels for 0%

profile of v3, /device:TPU:1, one launch (start us, length us, event | category | flops | bytes accessed | tf_op | source)
XLA Modules:
  0.0 57.6 jit_solution(11759464977170497563)
XLA Ops:
  0.7 6.8 %beams.1 = (f32[32,32,128]{2,1,0:T(8,128)S(1)}, f32[32,32,128]{2,1,0:T(8,128)S(1)}) custom-call(s32[1]{0:T(128)} %bitcast.side, s32[1]{0:T(128)} %bitcast.1.row, s32[1]{0:T(128)S(6)} %copy.9.live, s32[1,2,16]{2,1,0:T(2,128)} %bitcast.8, s32[1,16]{1,0:T(1,128)} %fanout_in.1, s32[32]{0:T(128)} %owned_in.1, bf16[2,64,16,2048]{3,2,1,0:T(8,128)(2,1)} %rf_in.1, ...), custom_call_target="tpu_custom_call" | custom-call | tf_op jit(solution)/shard_map/beams/pallas_call | solution.py:175
  7.5 7.5 %collective-permute-start = (f32[32,32,128]{2,1,0:T(8,128)S(1)}, f32[32,32,128]{2,1,0:T(8,128)S(1)}, u32[]{:S(2)}, u32[]{:S(2)}) collective-permute-start(f32[32,32,128]{2,1,0:T(8,128)S(1)} %get-tuple-element.8), channel_id=1, source_target_pairs={{0,128},{128,0},{1,129},{129,1},{2,130},{130,2},{3,131},{131,3},{4... | collective-permute-start | bytes 1572872 | tf_op jit(solution)/shard_map/ppermute | solution.py:226
  15.0 1.5 %collective-permute-done = f32[32,32,128]{2,1,0:T(8,128)S(1)} collective-permute-done((f32[32,32,128]{2,1,0:T(8,128)S(1)}, f32[32,32,128]{2,1,0:T(8,128)S(1)}, u32[]{:S(2)}, u32[]{:S(2)}) %collective-permute-start) | collective-permute-done | bytes 524320 | tf_op jit(solution)/shard_map/ppermute | solution.py:226
  16.6 0.1 slice_add_fusion.2
  16.6 0.1 collective-permute-start.1
  16.7 2.7 %collective-permute-start.3 = (f32[8,32,128]{2,1,0:T(8,128)S(1)}, f32[8,32,128]{2,1,0:T(8,128)S(1)}, u32[]{:S(2)}, u32[]{:S(2)}) collective-permute-start(f32[8,32,128]{2,1,0:T(8,128)S(1)} %get-tuple-element.10), channel_id=1, source_target_pairs={{0,96},{4,100},{8,104},{12,108},{16,112},{20,116},{24,120},{28,124... | collective-permute-start | bytes 393224 | tf_op jit(solution)/shard_map/ppermute | solution.py:233
  19.4 0.0 collective-permute-start.2
  19.4 3.2 %collective-permute-done.1 = f32[8,32,128]{2,1,0:T(8,128)S(1)} collective-permute-done((f32[8,32,128]{2,1,0:T(8,128)S(1)}, f32[8,32,128]{2,1,0:T(8,128)S(1)}, u32[]{:S(2)}, u32[]{:S(2)}) %collective-permute-start.1) | collective-permute-done | bytes 131104 | tf_op jit(solution)/shard_map/ppermute | solution.py:233
  22.6 1.9 %collective-permute-done.3 = f32[8,32,128]{2,1,0:T(8,128)S(1)} collective-permute-done((f32[8,32,128]{2,1,0:T(8,128)S(1)}, f32[8,32,128]{2,1,0:T(8,128)S(1)}, u32[]{:S(2)}, u32[]{:S(2)}) %collective-permute-start.3) | collective-permute-done | bytes 131104 | tf_op jit(solution)/shard_map/ppermute | solution.py:233
  24.5 0.2 collective-permute-done.2
  24.7 0.1 fusion.2
  24.7 20.3 %all_to_all.5 = f32[8,32,128]{2,1,0:T(8,128)S(1)} all-to-all(f32[8,32,128]{2,1,0:T(8,128)S(1)} %fusion.2), channel_id=1, replica_groups={{0,4,8,12,16,20,24,28},{32,36,40,44,48,52,56,60},{64,68,72,76,80,84,88,..., dimensions={0} | all-to-all | bytes 262144 | tf_op jit(solution)/shard_map/all_to_all | solution.py:237
  45.1 2.6 %collective-permute-start.6 = (f32[32,128]{1,0:T(8,128)S(1)}, f32[32,128]{1,0:T(8,128)S(1)}, u32[]{:S(2)}, u32[]{:S(2)}) collective-permute-start(f32[32,128]{1,0:T(8,128)S(1)} %reduce_sum.18), channel_id=1, source_target_pairs={{0,3},{1,0},{2,1},{3,2},{4,7},{5,4},{6,5},{7,6},{8,11},{9,8},{10,9... | collective-permute-start | bytes 49160 | tf_op jit(solution)/shard_map/ppermute | solution.py:241
  47.7 0.5 collective-permute-start.5
  48.1 0.7 %collective-permute-start.4 = (f32[32,128]{1,0:T(8,128)S(1)}, f32[32,128]{1,0:T(8,128)S(1)}, u32[]{:S(2)}, u32[]{:S(2)}) collective-permute-start(f32[32,128]{1,0:T(8,128)S(1)} %reduce_sum.18), channel_id=1, source_target_pairs={{0,1},{1,2},{2,3},{3,0},{4,5},{5,6},{6,7},{7,4},{8,9},{9,10},{10,1... | collective-permute-start | bytes 49160 | tf_op jit(solution)/shard_map/ppermute | solution.py:241
  48.8 0.0 collective-permute-done.6
  48.8 2.9 %collective-permute-done.5 = f32[32,128]{1,0:T(8,128)S(1)} collective-permute-done((f32[32,128]{1,0:T(8,128)S(1)}, f32[32,128]{1,0:T(8,128)S(1)}, u32[]{:S(2)}, u32[]{:S(2)}) %collective-permute-start.5) | collective-permute-done | bytes 16416 | tf_op jit(solution)/shard_map/ppermute | solution.py:241
  51.7 0.2 collective-permute-done.4
  52.0 4.3 %collective-permute-start.7 = (f32[1,128]{1,0:T(1,128)S(1)}, f32[1,128]{1,0:T(1,128)S(1)}, u32[]{:S(2)}, u32[]{:S(2)}) collective-permute-start(f32[1,128]{1,0:T(1,128)S(1)} %multiply_bitcast_fusion), channel_id=1, source_target_pairs={{0,128},{128,0},{1,129},{129,1},{2,130},{130,2},{3,131},{131,3},{4... | collective-permute-start | bytes 1544 | tf_op jit(solution)/shard_map/ppermute | solution.py:245
  56.3 0.8 %collective-permute-done.7 = f32[1,128]{1,0:T(1,128)S(1)} collective-permute-done((f32[1,128]{1,0:T(1,128)S(1)}, f32[1,128]{1,0:T(1,128)S(1)}, u32[]{:S(2)}, u32[]{:S(2)}) %collective-permute-start.7) | collective-permute-done | bytes 544 | tf_op jit(solution)/shard_map/ppermute | solution.py:245
  57.1 0.5 fusion.3
  (3 shorter events, 0.0 us)
Async XLA Ops:
  7.5 9.1 %collective-permute-start = (f32[32,32,128]{2,1,0:T(8,128)S(1)}, f32[32,32,128]{2,1,0:T(8,128)S(1)}, u32[]{:S(2)}, u32[]{:S(2)}) collective-permute-start(f32[32,32,128]{2,1,0:T(8,128)S(1)} %get-tuple-element.8), channel_id=1, source_target_pairs={{0,128},{128,0},{1,129},{129,1},{2,130},{130,2},{3,131},{131,3},{4... | collective-permute-start | bytes 1572872 | tf_op jit(solution)/shard_map/ppermute | solution.py:226
  16.6 6.0 %collective-permute-start.1 = (f32[8,32,128]{2,1,0:T(8,128)S(1)}, f32[8,32,128]{2,1,0:T(8,128)S(1)}, u32[]{:S(2)}, u32[]{:S(2)}) collective-permute-start(f32[8,32,128]{2,1,0:T(8,128)S(1)} %get-tuple-element.9), channel_id=1, source_target_pairs={{0,32},{4,36},{8,40},{12,44},{16,48},{20,52},{24,56},{28,60},{32,6... | collective-permute-start | bytes 393224 | tf_op jit(solution)/shard_map/ppermute | solution.py:233
  16.7 7.8 %collective-permute-start.3 = (f32[8,32,128]{2,1,0:T(8,128)S(1)}, f32[8,32,128]{2,1,0:T(8,128)S(1)}, u32[]{:S(2)}, u32[]{:S(2)}) collective-permute-start(f32[8,32,128]{2,1,0:T(8,128)S(1)} %get-tuple-element.10), channel_id=1, source_target_pairs={{0,96},{4,100},{8,104},{12,108},{16,112},{20,116},{24,120},{28,124... | collective-permute-start | bytes 393224 | tf_op jit(solution)/shard_map/ppermute | solution.py:233
  19.4 5.3 %collective-permute-start.2 = (f32[8,32,128]{2,1,0:T(8,128)S(1)}, f32[8,32,128]{2,1,0:T(8,128)S(1)}, u32[]{:S(2)}, u32[]{:S(2)}) collective-permute-start(f32[8,32,128]{2,1,0:T(8,128)S(1)} %get-tuple-element.11), channel_id=1, source_target_pairs={{0,64},{4,68},{8,72},{12,76},{16,80},{20,84},{24,88},{28,92},{32,9... | collective-permute-start | bytes 393224 | tf_op jit(solution)/shard_map/ppermute | solution.py:233
  45.1 3.7 %collective-permute-start.6 = (f32[32,128]{1,0:T(8,128)S(1)}, f32[32,128]{1,0:T(8,128)S(1)}, u32[]{:S(2)}, u32[]{:S(2)}) collective-permute-start(f32[32,128]{1,0:T(8,128)S(1)} %reduce_sum.18), channel_id=1, source_target_pairs={{0,3},{1,0},{2,1},{3,2},{4,7},{5,4},{6,5},{7,6},{8,11},{9,8},{10,9... | collective-permute-start | bytes 49160 | tf_op jit(solution)/shard_map/ppermute | solution.py:241
  47.7 4.1 %collective-permute-start.5 = (f32[32,128]{1,0:T(8,128)S(1)}, f32[32,128]{1,0:T(8,128)S(1)}, u32[]{:S(2)}, u32[]{:S(2)}) collective-permute-start(f32[32,128]{1,0:T(8,128)S(1)} %reduce_sum.18), channel_id=1, source_target_pairs={{0,2},{1,3},{2,0},{3,1},{4,6},{5,7},{6,4},{7,5},{8,10},{9,11},{10,... | collective-permute-start | bytes 49160 | tf_op jit(solution)/shard_map/ppermute | solution.py:241
  48.1 3.8 %collective-permute-start.4 = (f32[32,128]{1,0:T(8,128)S(1)}, f32[32,128]{1,0:T(8,128)S(1)}, u32[]{:S(2)}, u32[]{:S(2)}) collective-permute-start(f32[32,128]{1,0:T(8,128)S(1)} %reduce_sum.18), channel_id=1, source_target_pairs={{0,1},{1,2},{2,3},{3,0},{4,5},{5,6},{6,7},{7,4},{8,9},{9,10},{10,1... | collective-permute-start | bytes 49160 | tf_op jit(solution)/shard_map/ppermute | solution.py:241
  52.0 5.1 %collective-permute-start.7 = (f32[1,128]{1,0:T(1,128)S(1)}, f32[1,128]{1,0:T(1,128)S(1)}, u32[]{:S(2)}, u32[]{:S(2)}) collective-permute-start(f32[1,128]{1,0:T(1,128)S(1)} %multiply_bitcast_fusion), channel_id=1, source_target_pairs={{0,128},{128,0},{1,129},{129,1},{2,130},{130,2},{3,131},{131,3},{4... | collective-permute-start | bytes 1544 | tf_op jit(solution)/shard_map/ppermute | solution.py:245

commit v4 on v3

v4 whole, which is shorter than its diff:
```python
import jax
import jax.numpy as jnp
from jax import lax
from jax.experimental import pallas as pl
from jax.experimental.pallas import tpu as pltpu
from jax.sharding import PartitionSpec as P

LANES = 128
SUBLANES = 8
STEP = 16
ROWS = 4
BLOCK = 256
GROUP = 4


def beam_kernel(
    side, row, live, offsets_in, fanout_in, owned_in, rf_in, taps_in, weights_in, apod_in,
    keep, send,
    offsets, fanout, owned, place, taps, apod, rf, weights,
    toeplitz, filtered, small_sems, rf_sems, weight_sems,
):
    waves, frames, elems, samples = rf.shape
    slots, depth, voxels = weights.shape
    window = depth // elems
    history = taps.shape[1]
    half = frames // 2
    tiles = owned.shape[0]
    chunks = frames // STEP
    count = live[0]
    rounds = lax.div(count + GROUP - 1, GROUP)
    needed = rounds * GROUP
    small = [
        pltpu.make_async_copy(source, target, small_sems.at[i])
        for i, (source, target) in enumerate(
            [
                (offsets_in, offsets), (fanout_in, fanout), (owned_in, owned),
                (taps_in, taps), (apod_in, apod),
            ]
        )
    ]

    def rf_copy(unit):
        wave, chunk = lax.div(unit, chunks), lax.rem(unit, chunks)
        span = pl.ds(chunk * STEP, STEP)
        return pltpu.make_async_copy(
            rf_in.at[wave, span], rf.at[wave, span], rf_sems.at[unit]
        )

    def weight_copy(slot):
        return pltpu.make_async_copy(weights_in.at[0, slot], weights.at[slot], weight_sems.at[slot])

    for copy in small:
        copy.start()
    for unit in range(4):
        rf_copy(unit).start()
    keep[...] = jnp.zeros_like(keep)
    send[...] = jnp.zeros_like(send)
    for copy in small:
        copy.wait()
    width = 2 * BLOCK
    line = jnp.concatenate(
        [
            jnp.zeros((1, history), jnp.float32),
            taps[...].astype(jnp.float32),
            jnp.zeros((1, width - 2 * history), jnp.float32),
        ],
        axis=1,
    )
    flipped = jnp.concatenate([line[:, history:], line[:, :history]], axis=1)
    spread = jnp.broadcast_to(flipped, (BLOCK + history, width))
    toeplitz[...] = pltpu.roll(spread, width - history, 1, stride=1, stride_axis=0)[
        :, :BLOCK
    ].astype(jnp.bfloat16)

    columns = tiles // ROWS

    def note(index, carry):
        ahead = lax.rem(index // columns - row[0] + ROWS, ROWS)
        place[owned[index]] = ahead * columns + lax.rem(index, columns)
        return carry

    lax.fori_loop(0, tiles, note, 0)

    blocks = samples // BLOCK
    units = waves * chunks

    def spot(unit):
        wave, chunk = lax.div(unit, chunks), lax.rem(unit, chunks)
        return wave, pl.ds(pl.multiple_of(chunk * STEP, STEP), STEP)

    def filter_block(unit, block):
        wave, span = spot(unit)
        at = block * BLOCK
        back = min(at, history)
        cut = rf[wave, span, :, at - back : at + BLOCK].reshape(STEP * elems, back + BLOCK)
        lines = jnp.dot(
            cut, toeplitz[history - back :, :], preferred_element_type=jnp.float32
        ).astype(jnp.bfloat16)
        filtered[wave, :, span, at : at + BLOCK] = jnp.swapaxes(
            lines.reshape(STEP, elems, BLOCK), 0, 1
        )

    def two_units(index, carry):
        unit = 2 * index
        rf_copy(unit).wait()
        rf_copy(unit + 1).wait()
        for later in (unit + 4, unit + 5):

            @pl.when(later < units)
            def _():
                rf_copy(later).start()

        for slot in range(slots // 2):
            ahead = (index - units // 2 + 2) * (slots // 2) + slot

            @pl.when((ahead >= 0) & (ahead < needed))
            def _():
                weight_copy(ahead).start()

        for each in range(2):
            for block in range(blocks):
                filter_block(unit + each, block)
        return carry

    lax.fori_loop(0, units // 2, two_units, 0)

    lane_index = lax.broadcasted_iota(jnp.int32, (frames, LANES), 1)

    def do_slot(slot):
        cuts = []
        for wave in range(waves):
            start = offsets[0, wave, slot]
            tile = lax.div(start, LANES)
            shift = start - tile * LANES
            after = jnp.minimum(tile + 1, samples // LANES - 1)
            cuts.append(
                (
                    pl.multiple_of(tile * LANES, LANES),
                    pl.multiple_of(after * LANES, LANES),
                    lax.rem(LANES - shift, LANES),
                    lane_index >= shift,
                )
            )
        beam = jnp.zeros((waves * frames, voxels), jnp.float32)
        for elem in range(0, elems, 2):
            across = []
            for each in (elem, elem + 1):
                lines = []
                for wave, (tile, after, turn, inside) in enumerate(cuts):
                    joined = jnp.where(
                        inside,
                        filtered[wave, each, :, pl.ds(tile, LANES)],
                        filtered[wave, each, :, pl.ds(after, LANES)],
                    )
                    lines.append(pltpu.roll(joined, turn, 1))
                across.append(jnp.concatenate(lines, axis=0))
            beam += jnp.dot(
                jnp.concatenate(across, axis=1),
                weights[slot, elem * window : (elem + 2) * window, :],
                preferred_element_type=jnp.float32,
            )
        voxel_tile = fanout[0, slot]
        term = jnp.zeros((frames, voxels), jnp.float32)
        for wave in range(waves):
            term += apod[wave, pl.ds(voxel_tile, 1), :] * beam[wave * frames : (wave + 1) * frames]
        term -= jnp.sum(term, axis=0, keepdims=True) * (1.0 / frames)
        where = place[voxel_tile]
        alive = slot < count
        swap = side[0] == 1
        keep[where] = jnp.where(alive, jnp.where(swap, term[half:], term[:half]), keep[where])
        send[where] = jnp.where(alive, jnp.where(swap, term[:half], term[half:]), send[where])

    def some_slots(index, carry):
        for each in range(GROUP):
            weight_copy(GROUP * index + each).wait()
        for each in range(GROUP):
            do_slot(GROUP * index + each)
        return carry

    lax.fori_loop(0, rounds, some_slots, 0)


def local_images(side, row, rf, taps, weights, apod, fanout, live, offsets, owned, opts=()):
    waves, frames, elems, samples = rf.shape
    slots, depth, voxels = weights.shape[1:]
    history = taps.shape[0]
    tiles = owned.shape[0]
    image = jax.ShapeDtypeStruct((tiles, frames // 2, voxels), jnp.float32)
    smem = pl.BlockSpec(memory_space=pltpu.SMEM)
    hbm = pl.BlockSpec(memory_space=pltpu.HBM)
    vmem = pl.BlockSpec(memory_space=pltpu.VMEM)
    return pl.pallas_call(
        beam_kernel,
        out_shape=(image, image),
        in_specs=[smem, smem, smem] + [hbm] * 7,
        out_specs=[vmem, vmem],
        scratch_shapes=[
            pltpu.SMEM((1, waves, slots), jnp.int32),
            pltpu.SMEM((1, slots), jnp.int32),
            pltpu.SMEM((tiles,), jnp.int32),
            pltpu.SMEM((tiles,), jnp.int32),
            pltpu.VMEM((1, history), jnp.bfloat16),
            pltpu.VMEM(apod.shape, jnp.float32),
            pltpu.VMEM(rf.shape, jnp.bfloat16),
            pltpu.VMEM(weights.shape[1:], jnp.bfloat16),
            pltpu.VMEM((BLOCK + history, BLOCK), jnp.bfloat16),
            pltpu.VMEM((waves, elems, frames, samples), jnp.bfloat16),
            pltpu.SemaphoreType.DMA((5,)),
            pltpu.SemaphoreType.DMA((waves * (frames // STEP),)),
            pltpu.SemaphoreType.DMA((slots,)),
        ],
        compiler_params=pltpu.CompilerParams(vmem_limit_bytes=48 * 2**20),
        name="beams",
    )(
        side,
        row,
        live,
        *[
            pltpu.with_memory_space_constraint(array, pltpu.HBM)
            for array in (
                offsets.transpose(0, 2, 1), fanout, owned, rf, taps[None], weights, apod,
            )
        ],
    )


def on_device(
    rf_rows, filter_taps, interp_weights, apodization, fanout, live_slots, offsets, owned_tiles
):
    frames = rf_rows.shape[1]
    wave_groups = lax.axis_size("wave")
    tiles = lax.axis_size("tile")
    columns = tiles // ROWS
    side = lax.axis_index("section").astype(jnp.int32)[None]
    row = lax.div(lax.axis_index("tile").astype(jnp.int32), jnp.int32(columns))[None]
    keep, send = local_images(
        side, row, rf_rows, filter_taps, interp_weights, apodization, fanout, live_slots, offsets,
        owned_tiles,
    )
    swap = [(0, 1), (1, 0)]
    got = lax.ppermute(send, "section", swap)
    pairs = [
        keep[at * columns : (at + 1) * columns] + got[at * columns : (at + 1) * columns]
        for at in range(ROWS)
    ]
    line = pairs[0]
    for hop in range(1, ROWS):
        line = line + lax.ppermute(
            pairs[hop], "tile", [(i, (i + hop * columns) % tiles) for i in range(tiles)]
        )
    groups = [[at * columns + i for i in range(columns)] for at in range(ROWS)]
    parts = lax.all_to_all(line, "tile", 0, 0, axis_index_groups=groups, tiled=True)
    mine = jnp.sum(parts, axis=0)
    total = mine
    for hop in range(1, wave_groups):
        total = total + lax.ppermute(
            mine, "wave", [(i, (i + hop) % wave_groups) for i in range(wave_groups)]
        )
    power = jnp.sum(total * total, axis=0, keepdims=True) * (1.0 / frames)
    return power + lax.ppermute(power, "section", swap)


def solution(mesh):
    return jax.shard_map(
        on_device,
        mesh=mesh,
        in_specs=(
            P("wave", None, ("section", "tile"), None),
            P(),
            P(("section", "tile"), None, None, None),
            P("wave", None, None),
            P(("section", "tile"), None),
            P(("section", "tile")),
            P(("section", "tile"), None, "wave"),
            P(),
        ),
        out_specs=P("tile", None),
        check_vma=False,
    )
```

time: 57.8 us -> 56 us (0.969)
  blocking collectives: 20.3 us -> 16 us
  Pallas kernels: 6.8 us -> 9.42 us
  starting transfers between devices: 18.3 us -> 17.6 us
  waiting for transfers between devices: 10.8 us -> 11.4 us
    all_to_all x1, blocking collectives: 20.3 us -> 16 us  [on_device(): lax.all_to_all(line, 'tile', 0, 0, axis_index_groups=groups, tiled=True)]
    pallas_call x1, Pallas kernels: 6.8 us -> 9.42 us  [local_images(): pl.pallas_call(beam_kernel, out_shape=(image, image), in_specs=[smem, sme...]
    ppermute x1, starting transfers between devices: 7.55 us -> 6.22 us  [on_device(): got = lax.ppermute(send, 'section', swap)]
    ppermute x3, starting transfers between devices: 2.75 us -> 3.39 us  [on_device(): lax.ppermute(pairs[hop], 'tile', [(i, (i + hop * columns) % tiles) for i...]
  transfers between devices with their start and end apart: 8 -> 8, of which waited for: 7 -> 6; matrix products, arithmetic and copies ran while one was open for 0% -> 0% of each run, Pallas kernels for 0% -> 0%
where the time goes in v4:
time: 56 us; the launch traced here: 55.8 us
  starting transfers between devices  17.6 us (31%)
  blocking collectives  16 us (29%)
  waiting for transfers between devices  11.4 us (20%)
  Pallas kernels  9.42 us (17%)
  between operations  0.68 us (1%)
  other arithmetic  0.67 us (1%)
    all_to_all x1, blocking collectives, on_device(): lax.all_to_all(line, 'tile', 0, 0, axis_index_groups=groups, tiled=True)  16 us
    pallas_call x1, Pallas kernels, local_images(): pl.pallas_call(beam_kernel, out_shape=(image, image), in_specs=[smem, sme...  9.42 us
    ppermute x1, starting transfers between devices, on_device(): got = lax.ppermute(send, 'section', swap)  6.22 us
    ppermute x3, waiting for transfers between devices, on_device(): lax.ppermute(pairs[hop], 'tile', [(i, (i + hop * columns) % tiles) for i...  5.88 us
    ppermute x1, starting transfers between devices, on_device(): return power + lax.ppermute(power, 'section', swap)  4.32 us
    ppermute x3, starting transfers between devices, on_device(): lax.ppermute(mine, 'wave', [(i, (i + hop) % wave_groups) for i in range(w...  3.68 us
    ppermute x3, starting transfers between devices, on_device(): lax.ppermute(pairs[hop], 'tile', [(i, (i + hop * columns) % tiles) for i...  3.39 us
    ppermute x3, waiting for transfers between devices, on_device(): lax.ppermute(mine, 'wave', [(i, (i + hop) % wave_groups) for i in range(w...  3.17 us
  transfers between devices with their start and end apart: 8, of which 6 were waited for; matrix products, arithmetic and copies ran while one was open for 0% of the time, Pallas kernels for 0%

profile of v4, /device:TPU:1, one launch (start us, length us, event | category | flops | bytes accessed | tf_op | source)
XLA Modules:
  0.0 55.8 jit_solution(10591378343221590871)
XLA Ops:
  0.7 9.4 %beams.1 = (f32[32,32,128]{2,1,0:T(8,128)S(1)}, f32[32,32,128]{2,1,0:T(8,128)S(1)}) custom-call(s32[1]{0:T(128)} %bitcast.side, s32[1]{0:T(128)} %bitcast.1.row, s32[1]{0:T(128)S(6)} %copy.9.live, s32[1,2,16]{2,1,0:T(2,128)} %bitcast.8, s32[1,16]{1,0:T(1,128)} %fanout_in.1, s32[32]{0:T(128)} %owned_in.1, bf16[2,64,16,2048]{3,2,1,0:T(8,128)(2,1)} %rf_in.1, ...), custom_call_target="tpu_custom_call" | custom-call | tf_op jit(solution)/shard_map/beams/pallas_call | solution.py:192
  10.1 6.2 %collective-permute-start = (f32[32,32,128]{2,1,0:T(8,128)S(1)}, f32[32,32,128]{2,1,0:T(8,128)S(1)}, u32[]{:S(2)}, u32[]{:S(2)}) collective-permute-start(f32[32,32,128]{2,1,0:T(8,128)S(1)} %get-tuple-element.8), channel_id=1, source_target_pairs={{0,128},{128,0},{1,129},{129,1},{2,130},{130,2},{3,131},{131,3},{4... | collective-permute-start | bytes 1572872 | tf_op jit(solution)/shard_map/ppermute | solution.py:241
  16.3 1.5 %collective-permute-done = f32[32,32,128]{2,1,0:T(8,128)S(1)} collective-permute-done((f32[32,32,128]{2,1,0:T(8,128)S(1)}, f32[32,32,128]{2,1,0:T(8,128)S(1)}, u32[]{:S(2)}, u32[]{:S(2)}) %collective-permute-start) | collective-permute-done | bytes 524320 | tf_op jit(solution)/shard_map/ppermute | solution.py:241
  17.8 0.1 slice_add_fusion.2
  17.9 0.1 collective-permute-start.1
  18.0 2.7 %collective-permute-start.3 = (f32[8,32,128]{2,1,0:T(8,128)S(1)}, f32[8,32,128]{2,1,0:T(8,128)S(1)}, u32[]{:S(2)}, u32[]{:S(2)}) collective-permute-start(f32[8,32,128]{2,1,0:T(8,128)S(1)} %get-tuple-element.10), channel_id=1, source_target_pairs={{0,96},{4,100},{8,104},{12,108},{16,112},{20,116},{24,120},{28,124... | collective-permute-start | bytes 393224 | tf_op jit(solution)/shard_map/ppermute | solution.py:248
  20.7 0.6 %collective-permute-start.2 = (f32[8,32,128]{2,1,0:T(8,128)S(1)}, f32[8,32,128]{2,1,0:T(8,128)S(1)}, u32[]{:S(2)}, u32[]{:S(2)}) collective-permute-start(f32[8,32,128]{2,1,0:T(8,128)S(1)} %get-tuple-element.11), channel_id=1, source_target_pairs={{0,64},{4,68},{8,72},{12,76},{16,80},{20,84},{24,88},{28,92},{32,9... | collective-permute-start | bytes 393224 | tf_op jit(solution)/shard_map/ppermute | solution.py:248
  21.3 2.6 %collective-permute-done.1 = f32[8,32,128]{2,1,0:T(8,128)S(1)} collective-permute-done((f32[8,32,128]{2,1,0:T(8,128)S(1)}, f32[8,32,128]{2,1,0:T(8,128)S(1)}, u32[]{:S(2)}, u32[]{:S(2)}) %collective-permute-start.1) | collective-permute-done | bytes 131104 | tf_op jit(solution)/shard_map/ppermute | solution.py:248
  23.9 0.0 collective-permute-done.3
  23.9 3.3 %collective-permute-done.2 = f32[8,32,128]{2,1,0:T(8,128)S(1)} collective-permute-done((f32[8,32,128]{2,1,0:T(8,128)S(1)}, f32[8,32,128]{2,1,0:T(8,128)S(1)}, u32[]{:S(2)}, u32[]{:S(2)}) %collective-permute-start.2) | collective-permute-done | bytes 131104 | tf_op jit(solution)/shard_map/ppermute | solution.py:248
  27.2 0.1 fusion.2
  27.2 16.0 %all_to_all.5 = f32[8,32,128]{2,1,0:T(8,128)S(1)} all-to-all(f32[8,32,128]{2,1,0:T(8,128)S(1)} %fusion.2), channel_id=1, replica_groups={{0,4,8,12,16,20,24,28},{32,36,40,44,48,52,56,60},{64,68,72,76,80,84,88,..., dimensions={0} | all-to-all | bytes 262144 | tf_op jit(solution)/shard_map/all_to_all | solution.py:252
  43.3 2.5 %collective-permute-start.6 = (f32[32,128]{1,0:T(8,128)S(1)}, f32[32,128]{1,0:T(8,128)S(1)}, u32[]{:S(2)}, u32[]{:S(2)}) collective-permute-start(f32[32,128]{1,0:T(8,128)S(1)} %reduce_sum.18), channel_id=1, source_target_pairs={{0,3},{1,0},{2,1},{3,2},{4,7},{5,4},{6,5},{7,6},{8,11},{9,8},{10,9... | collective-permute-start | bytes 49160 | tf_op jit(solution)/shard_map/ppermute | solution.py:256
  45.8 0.5 collective-permute-start.5
  46.3 0.6 %collective-permute-start.4 = (f32[32,128]{1,0:T(8,128)S(1)}, f32[32,128]{1,0:T(8,128)S(1)}, u32[]{:S(2)}, u32[]{:S(2)}) collective-permute-start(f32[32,128]{1,0:T(8,128)S(1)} %reduce_sum.18), channel_id=1, source_target_pairs={{0,1},{1,2},{2,3},{3,0},{4,5},{5,6},{6,7},{7,4},{8,9},{9,10},{10,1... | collective-permute-start | bytes 49160 | tf_op jit(solution)/shard_map/ppermute | solution.py:256
  47.0 0.0 collective-permute-done.6
  47.0 2.9 %collective-permute-done.5 = f32[32,128]{1,0:T(8,128)S(1)} collective-permute-done((f32[32,128]{1,0:T(8,128)S(1)}, f32[32,128]{1,0:T(8,128)S(1)}, u32[]{:S(2)}, u32[]{:S(2)}) %collective-permute-start.5) | collective-permute-done | bytes 16416 | tf_op jit(solution)/shard_map/ppermute | solution.py:256
  49.9 0.2 collective-permute-done.4
  50.2 4.3 %collective-permute-start.7 = (f32[1,128]{1,0:T(1,128)S(1)}, f32[1,128]{1,0:T(1,128)S(1)}, u32[]{:S(2)}, u32[]{:S(2)}) collective-permute-start(f32[1,128]{1,0:T(1,128)S(1)} %multiply_bitcast_fusion), channel_id=1, source_target_pairs={{0,128},{128,0},{1,129},{129,1},{2,130},{130,2},{3,131},{131,3},{4... | collective-permute-start | bytes 1544 | tf_op jit(solution)/shard_map/ppermute | solution.py:260
  54.5 0.8 %collective-permute-done.7 = f32[1,128]{1,0:T(1,128)S(1)} collective-permute-done((f32[1,128]{1,0:T(1,128)S(1)}, f32[1,128]{1,0:T(1,128)S(1)}, u32[]{:S(2)}, u32[]{:S(2)}) %collective-permute-start.7) | collective-permute-done | bytes 544 | tf_op jit(solution)/shard_map/ppermute | solution.py:260
  55.3 0.5 fusion.3
  (3 shorter events, 0.0 us)
Async XLA Ops:
  10.1 7.8 %collective-permute-start = (f32[32,32,128]{2,1,0:T(8,128)S(1)}, f32[32,32,128]{2,1,0:T(8,128)S(1)}, u32[]{:S(2)}, u32[]{:S(2)}) collective-permute-start(f32[32,32,128]{2,1,0:T(8,128)S(1)} %get-tuple-element.8), channel_id=1, source_target_pairs={{0,128},{128,0},{1,129},{129,1},{2,130},{130,2},{3,131},{131,3},{4... | collective-permute-start | bytes 1572872 | tf_op jit(solution)/shard_map/ppermute | solution.py:241
  17.9 6.0 %collective-permute-start.1 = (f32[8,32,128]{2,1,0:T(8,128)S(1)}, f32[8,32,128]{2,1,0:T(8,128)S(1)}, u32[]{:S(2)}, u32[]{:S(2)}) collective-permute-start(f32[8,32,128]{2,1,0:T(8,128)S(1)} %get-tuple-element.9), channel_id=1, source_target_pairs={{0,32},{4,36},{8,40},{12,44},{16,48},{20,52},{24,56},{28,60},{32,6... | collective-permute-start | bytes 393224 | tf_op jit(solution)/shard_map/ppermute | solution.py:248
  18.0 5.9 %collective-permute-start.3 = (f32[8,32,128]{2,1,0:T(8,128)S(1)}, f32[8,32,128]{2,1,0:T(8,128)S(1)}, u32[]{:S(2)}, u32[]{:S(2)}) collective-permute-start(f32[8,32,128]{2,1,0:T(8,128)S(1)} %get-tuple-element.10), channel_id=1, source_target_pairs={{0,96},{4,100},{8,104},{12,108},{16,112},{20,116},{24,120},{28,124... | collective-permute-start | bytes 393224 | tf_op jit(solution)/shard_map/ppermute | solution.py:248
  20.7 6.5 %collective-permute-start.2 = (f32[8,32,128]{2,1,0:T(8,128)S(1)}, f32[8,32,128]{2,1,0:T(8,128)S(1)}, u32[]{:S(2)}, u32[]{:S(2)}) collective-permute-start(f32[8,32,128]{2,1,0:T(8,128)S(1)} %get-tuple-element.11), channel_id=1, source_target_pairs={{0,64},{4,68},{8,72},{12,76},{16,80},{20,84},{24,88},{28,92},{32,9... | collective-permute-start | bytes 393224 | tf_op jit(solution)/shard_map/ppermute | solution.py:248
  43.3 3.7 %collective-permute-start.6 = (f32[32,128]{1,0:T(8,128)S(1)}, f32[32,128]{1,0:T(8,128)S(1)}, u32[]{:S(2)}, u32[]{:S(2)}) collective-permute-start(f32[32,128]{1,0:T(8,128)S(1)} %reduce_sum.18), channel_id=1, source_target_pairs={{0,3},{1,0},{2,1},{3,2},{4,7},{5,4},{6,5},{7,6},{8,11},{9,8},{10,9... | collective-permute-start | bytes 49160 | tf_op jit(solution)/shard_map/ppermute | solution.py:256
  45.8 4.1 %collective-permute-start.5 = (f32[32,128]{1,0:T(8,128)S(1)}, f32[32,128]{1,0:T(8,128)S(1)}, u32[]{:S(2)}, u32[]{:S(2)}) collective-permute-start(f32[32,128]{1,0:T(8,128)S(1)} %reduce_sum.18), channel_id=1, source_target_pairs={{0,2},{1,3},{2,0},{3,1},{4,6},{5,7},{6,4},{7,5},{8,10},{9,11},{10,... | collective-permute-start | bytes 49160 | tf_op jit(solution)/shard_map/ppermute | solution.py:256
  46.3 3.8 %collective-permute-start.4 = (f32[32,128]{1,0:T(8,128)S(1)}, f32[32,128]{1,0:T(8,128)S(1)}, u32[]{:S(2)}, u32[]{:S(2)}) collective-permute-start(f32[32,128]{1,0:T(8,128)S(1)} %reduce_sum.18), channel_id=1, source_target_pairs={{0,1},{1,2},{2,3},{3,0},{4,5},{5,6},{6,7},{7,4},{8,9},{9,10},{10,1... | collective-permute-start | bytes 49160 | tf_op jit(solution)/shard_map/ppermute | solution.py:256
  50.2 5.1 %collective-permute-start.7 = (f32[1,128]{1,0:T(1,128)S(1)}, f32[1,128]{1,0:T(1,128)S(1)}, u32[]{:S(2)}, u32[]{:S(2)}) collective-permute-start(f32[1,128]{1,0:T(1,128)S(1)} %multiply_bitcast_fusion), channel_id=1, source_target_pairs={{0,128},{128,0},{1,129},{129,1},{2,130},{130,2},{3,131},{131,3},{4... | collective-permute-start | bytes 1544 | tf_op jit(solution)/shard_map/ppermute | solution.py:260

commit v5 on v4

--- a/solution.py
+++ b/solution.py
@@ -51,7 +51,7 @@
 
     for copy in small:
         copy.start()
-    for unit in range(4):
+    for unit in range(2):
         rf_copy(unit).start()
     keep[...] = jnp.zeros_like(keep)
     send[...] = jnp.zeros_like(send)
@@ -122,6 +122,8 @@
                 filter_block(unit + each, block)
         return carry
 
+    for unit in range(2, 4):
+        rf_copy(unit).start()
     lax.fori_loop(0, units // 2, two_units, 0)
 
     lane_index = lax.broadcasted_iota(jnp.int32, (frames, LANES), 1)
@@ -180,7 +182,7 @@
     lax.fori_loop(0, rounds, some_slots, 0)
 
 
-def local_images(side, row, rf, taps, weights, apod, fanout, live, offsets, owned, opts=()):
+def local_images(side, row, rf, taps, weights, apod, fanout, live, offsets, owned):
     waves, frames, elems, samples = rf.shape
     slots, depth, voxels = weights.shape[1:]
     history = taps.shape[0]

time: 56 us -> 55.2 us (0.986)
  starting transfers between devices: 17.6 us -> 15 us
  Pallas kernels: 9.42 us -> 11.8 us
  waiting for transfers between devices: 11.4 us -> 9.75 us
  blocking collectives: 16 us -> 17.6 us
    ppermute x1, starting transfers between devices: 6.22 us -> 3.31 us  [on_device(): got = lax.ppermute(send, 'section', swap)]
    pallas_call x1, Pallas kernels: 9.42 us -> 11.8 us  [local_images(): pl.pallas_call(beam_kernel, out_shape=(image, image), in_specs=[smem, sme...]
    ppermute x3, waiting for transfers between devices: 5.88 us -> 4.18 us  [on_device(): lax.ppermute(pairs[hop], 'tile', [(i, (i + hop * columns) % tiles) for i...]
    all_to_all x1, blocking collectives: 16 us -> 17.6 us  [on_device(): lax.all_to_all(line, 'tile', 0, 0, axis_index_groups=groups, tiled=True)]
where the time goes in v5:
time: 55.2 us; the launch traced here: 55.5 us
  blocking collectives  17.6 us (32%)
  starting transfers between devices  15 us (27%)
  Pallas kernels  11.8 us (21%)
  waiting for transfers between devices  9.75 us (18%)
  between operations  0.68 us (1%)
  other arithmetic  0.67 us (1%)
    all_to_all x1, blocking collectives, on_device(): lax.all_to_all(line, 'tile', 0, 0, axis_index_groups=groups, tiled=True)  17.6 us
    pallas_call x1, Pallas kernels, local_images(): pl.pallas_call(beam_kernel, out_shape=(image, image), in_specs=[smem, sme...  11.8 us
    ppermute x3, waiting for transfers between devices, on_device(): lax.ppermute(pairs[hop], 'tile', [(i, (i + hop * columns) % tiles) for i...  4.18 us
    ppermute x1, starting transfers between devices, on_device(): return power + lax.ppermute(power, 'section', swap)  4.17 us
    ppermute x3, starting transfers between devices, on_device(): lax.ppermute(pairs[hop], 'tile', [(i, (i + hop * columns) % tiles) for i...  3.89 us
    ppermute x3, starting transfers between devices, on_device(): lax.ppermute(mine, 'wave', [(i, (i + hop) % wave_groups) for i in range(w...  3.66 us
    ppermute x1, starting transfers between devices, on_device(): got = lax.ppermute(send, 'section', swap)  3.31 us
    ppermute x3, waiting for transfers between devices, on_device(): lax.ppermute(mine, 'wave', [(i, (i + hop) % wave_groups) for i in range(w...  3.21 us
  transfers between devices with their start and end apart: 8, of which 6 were waited for; matrix products, arithmetic and copies ran while one was open for 0% of the time, Pallas kernels for 0%

profile of v5, /device:TPU:1, one launch (start us, length us, event | category | flops | bytes accessed | tf_op | source)
XLA Modules:
  0.0 55.5 jit_solution(7110060888651206865)
XLA Ops:
  0.7 11.8 %beams.1 = (f32[32,32,128]{2,1,0:T(8,128)S(1)}, f32[32,32,128]{2,1,0:T(8,128)S(1)}) custom-call(s32[1]{0:T(128)} %bitcast.side, s32[1]{0:T(128)} %bitcast.1.row, s32[1]{0:T(128)S(6)} %copy.9.live, s32[1,2,16]{2,1,0:T(2,128)} %bitcast.8, s32[1,16]{1,0:T(1,128)} %fanout_in.1, s32[32]{0:T(128)} %owned_in.1, bf16[2,64,16,2048]{3,2,1,0:T(8,128)(2,1)} %rf_in.1, ...), custom_call_target="tpu_custom_call" | custom-call | tf_op jit(solution)/shard_map/beams/pallas_call | solution.py:194
  12.5 3.3 %collective-permute-start = (f32[32,32,128]{2,1,0:T(8,128)S(1)}, f32[32,32,128]{2,1,0:T(8,128)S(1)}, u32[]{:S(2)}, u32[]{:S(2)}) collective-permute-start(f32[32,32,128]{2,1,0:T(8,128)S(1)} %get-tuple-element.8), channel_id=1, source_target_pairs={{0,128},{128,0},{1,129},{129,1},{2,130},{130,2},{3,131},{131,3},{4... | collective-permute-start | bytes 1572872 | tf_op jit(solution)/shard_map/ppermute | solution.py:243
  15.8 1.5 %collective-permute-done = f32[32,32,128]{2,1,0:T(8,128)S(1)} collective-permute-done((f32[32,32,128]{2,1,0:T(8,128)S(1)}, f32[32,32,128]{2,1,0:T(8,128)S(1)}, u32[]{:S(2)}, u32[]{:S(2)}) %collective-permute-start) | collective-permute-done | bytes 524320 | tf_op jit(solution)/shard_map/ppermute | solution.py:243
  17.3 0.1 slice_add_fusion.2
  17.4 1.1 %collective-permute-start.1 = (f32[8,32,128]{2,1,0:T(8,128)S(1)}, f32[8,32,128]{2,1,0:T(8,128)S(1)}, u32[]{:S(2)}, u32[]{:S(2)}) collective-permute-start(f32[8,32,128]{2,1,0:T(8,128)S(1)} %get-tuple-element.9), channel_id=1, source_target_pairs={{0,32},{4,36},{8,40},{12,44},{16,48},{20,52},{24,56},{28,60},{32,6... | collective-permute-start | bytes 393224 | tf_op jit(solution)/shard_map/ppermute | solution.py:250
  18.5 1.7 %collective-permute-start.3 = (f32[8,32,128]{2,1,0:T(8,128)S(1)}, f32[8,32,128]{2,1,0:T(8,128)S(1)}, u32[]{:S(2)}, u32[]{:S(2)}) collective-permute-start(f32[8,32,128]{2,1,0:T(8,128)S(1)} %get-tuple-element.10), channel_id=1, source_target_pairs={{0,96},{4,100},{8,104},{12,108},{16,112},{20,116},{24,120},{28,124... | collective-permute-start | bytes 393224 | tf_op jit(solution)/shard_map/ppermute | solution.py:250
  20.2 1.1 %collective-permute-start.2 = (f32[8,32,128]{2,1,0:T(8,128)S(1)}, f32[8,32,128]{2,1,0:T(8,128)S(1)}, u32[]{:S(2)}, u32[]{:S(2)}) collective-permute-start(f32[8,32,128]{2,1,0:T(8,128)S(1)} %get-tuple-element.11), channel_id=1, source_target_pairs={{0,64},{4,68},{8,72},{12,76},{16,80},{20,84},{24,88},{28,92},{32,9... | collective-permute-start | bytes 393224 | tf_op jit(solution)/shard_map/ppermute | solution.py:250
  21.3 2.1 %collective-permute-done.1 = f32[8,32,128]{2,1,0:T(8,128)S(1)} collective-permute-done((f32[8,32,128]{2,1,0:T(8,128)S(1)}, f32[8,32,128]{2,1,0:T(8,128)S(1)}, u32[]{:S(2)}, u32[]{:S(2)}) %collective-permute-start.1) | collective-permute-done | bytes 131104 | tf_op jit(solution)/shard_map/ppermute | solution.py:250
  23.4 0.0 collective-permute-done.3
  23.4 2.1 %collective-permute-done.2 = f32[8,32,128]{2,1,0:T(8,128)S(1)} collective-permute-done((f32[8,32,128]{2,1,0:T(8,128)S(1)}, f32[8,32,128]{2,1,0:T(8,128)S(1)}, u32[]{:S(2)}, u32[]{:S(2)}) %collective-permute-start.2) | collective-permute-done | bytes 131104 | tf_op jit(solution)/shard_map/ppermute | solution.py:250
  25.5 0.1 fusion.2
  25.5 17.6 %all_to_all.5 = f32[8,32,128]{2,1,0:T(8,128)S(1)} all-to-all(f32[8,32,128]{2,1,0:T(8,128)S(1)} %fusion.2), channel_id=1, replica_groups={{0,4,8,12,16,20,24,28},{32,36,40,44,48,52,56,60},{64,68,72,76,80,84,88,..., dimensions={0} | all-to-all | bytes 262144 | tf_op jit(solution)/shard_map/all_to_all | solution.py:254
  43.1 2.5 %collective-permute-start.6 = (f32[32,128]{1,0:T(8,128)S(1)}, f32[32,128]{1,0:T(8,128)S(1)}, u32[]{:S(2)}, u32[]{:S(2)}) collective-permute-start(f32[32,128]{1,0:T(8,128)S(1)} %reduce_sum.18), channel_id=1, source_target_pairs={{0,3},{1,0},{2,1},{3,2},{4,7},{5,4},{6,5},{7,6},{8,11},{9,8},{10,9... | collective-permute-start | bytes 49160 | tf_op jit(solution)/shard_map/ppermute | solution.py:258
  45.6 0.6 %collective-permute-start.5 = (f32[32,128]{1,0:T(8,128)S(1)}, f32[32,128]{1,0:T(8,128)S(1)}, u32[]{:S(2)}, u32[]{:S(2)}) collective-permute-start(f32[32,128]{1,0:T(8,128)S(1)} %reduce_sum.18), channel_id=1, source_target_pairs={{0,2},{1,3},{2,0},{3,1},{4,6},{5,7},{6,4},{7,5},{8,10},{9,11},{10,... | collective-permute-start | bytes 49160 | tf_op jit(solution)/shard_map/ppermute | solution.py:258
  46.2 0.6 %collective-permute-start.4 = (f32[32,128]{1,0:T(8,128)S(1)}, f32[32,128]{1,0:T(8,128)S(1)}, u32[]{:S(2)}, u32[]{:S(2)}) collective-permute-start(f32[32,128]{1,0:T(8,128)S(1)} %reduce_sum.18), channel_id=1, source_target_pairs={{0,1},{1,2},{2,3},{3,0},{4,5},{5,6},{6,7},{7,4},{8,9},{9,10},{10,1... | collective-permute-start | bytes 49160 | tf_op jit(solution)/shard_map/ppermute | solution.py:258
  46.8 0.0 collective-permute-done.6
  46.8 2.9 %collective-permute-done.5 = f32[32,128]{1,0:T(8,128)S(1)} collective-permute-done((f32[32,128]{1,0:T(8,128)S(1)}, f32[32,128]{1,0:T(8,128)S(1)}, u32[]{:S(2)}, u32[]{:S(2)}) %collective-permute-start.5) | collective-permute-done | bytes 16416 | tf_op jit(solution)/shard_map/ppermute | solution.py:258
  49.7 0.3 collective-permute-done.4
  50.0 4.2 %collective-permute-start.7 = (f32[1,128]{1,0:T(1,128)S(1)}, f32[1,128]{1,0:T(1,128)S(1)}, u32[]{:S(2)}, u32[]{:S(2)}) collective-permute-start(f32[1,128]{1,0:T(1,128)S(1)} %multiply_bitcast_fusion), channel_id=1, source_target_pairs={{0,128},{128,0},{1,129},{129,1},{2,130},{130,2},{3,131},{131,3},{4... | collective-permute-start | bytes 1544 | tf_op jit(solution)/shard_map/ppermute | solution.py:262
  54.2 0.8 %collective-permute-done.7 = f32[1,128]{1,0:T(1,128)S(1)} collective-permute-done((f32[1,128]{1,0:T(1,128)S(1)}, f32[1,128]{1,0:T(1,128)S(1)}, u32[]{:S(2)}, u32[]{:S(2)}) %collective-permute-start.7) | collective-permute-done | bytes 544 | tf_op jit(solution)/shard_map/ppermute | solution.py:262
  55.0 0.5 fusion.3
  (3 shorter events, 0.0 us)
Async XLA Ops:
  12.5 4.9 %collective-permute-start = (f32[32,32,128]{2,1,0:T(8,128)S(1)}, f32[32,32,128]{2,1,0:T(8,128)S(1)}, u32[]{:S(2)}, u32[]{:S(2)}) collective-permute-start(f32[32,32,128]{2,1,0:T(8,128)S(1)} %get-tuple-element.8), channel_id=1, source_target_pairs={{0,128},{128,0},{1,129},{129,1},{2,130},{130,2},{3,131},{131,3},{4... | collective-permute-start | bytes 1572872 | tf_op jit(solution)/shard_map/ppermute | solution.py:243
  17.4 6.0 %collective-permute-start.1 = (f32[8,32,128]{2,1,0:T(8,128)S(1)}, f32[8,32,128]{2,1,0:T(8,128)S(1)}, u32[]{:S(2)}, u32[]{:S(2)}) collective-permute-start(f32[8,32,128]{2,1,0:T(8,128)S(1)} %get-tuple-element.9), channel_id=1, source_target_pairs={{0,32},{4,36},{8,40},{12,44},{16,48},{20,52},{24,56},{28,60},{32,6... | collective-permute-start | bytes 393224 | tf_op jit(solution)/shard_map/ppermute | solution.py:250
  18.5 4.9 %collective-permute-start.3 = (f32[8,32,128]{2,1,0:T(8,128)S(1)}, f32[8,32,128]{2,1,0:T(8,128)S(1)}, u32[]{:S(2)}, u32[]{:S(2)}) collective-permute-start(f32[8,32,128]{2,1,0:T(8,128)S(1)} %get-tuple-element.10), channel_id=1, source_target_pairs={{0,96},{4,100},{8,104},{12,108},{16,112},{20,116},{24,120},{28,124... | collective-permute-start | bytes 393224 | tf_op jit(solution)/shard_map/ppermute | solution.py:250
  20.2 5.3 %collective-permute-start.2 = (f32[8,32,128]{2,1,0:T(8,128)S(1)}, f32[8,32,128]{2,1,0:T(8,128)S(1)}, u32[]{:S(2)}, u32[]{:S(2)}) collective-permute-start(f32[8,32,128]{2,1,0:T(8,128)S(1)} %get-tuple-element.11), channel_id=1, source_target_pairs={{0,64},{4,68},{8,72},{12,76},{16,80},{20,84},{24,88},{28,92},{32,9... | collective-permute-start | bytes 393224 | tf_op jit(solution)/shard_map/ppermute | solution.py:250
  43.1 3.7 %collective-permute-start.6 = (f32[32,128]{1,0:T(8,128)S(1)}, f32[32,128]{1,0:T(8,128)S(1)}, u32[]{:S(2)}, u32[]{:S(2)}) collective-permute-start(f32[32,128]{1,0:T(8,128)S(1)} %reduce_sum.18), channel_id=1, source_target_pairs={{0,3},{1,0},{2,1},{3,2},{4,7},{5,4},{6,5},{7,6},{8,11},{9,8},{10,9... | collective-permute-start | bytes 49160 | tf_op jit(solution)/shard_map/ppermute | solution.py:258
  45.6 4.1 %collective-permute-start.5 = (f32[32,128]{1,0:T(8,128)S(1)}, f32[32,128]{1,0:T(8,128)S(1)}, u32[]{:S(2)}, u32[]{:S(2)}) collective-permute-start(f32[32,128]{1,0:T(8,128)S(1)} %reduce_sum.18), channel_id=1, source_target_pairs={{0,2},{1,3},{2,0},{3,1},{4,6},{5,7},{6,4},{7,5},{8,10},{9,11},{10,... | collective-permute-start | bytes 49160 | tf_op jit(solution)/shard_map/ppermute | solution.py:258
  46.2 3.8 %collective-permute-start.4 = (f32[32,128]{1,0:T(8,128)S(1)}, f32[32,128]{1,0:T(8,128)S(1)}, u32[]{:S(2)}, u32[]{:S(2)}) collective-permute-start(f32[32,128]{1,0:T(8,128)S(1)} %reduce_sum.18), channel_id=1, source_target_pairs={{0,1},{1,2},{2,3},{3,0},{4,5},{5,6},{6,7},{7,4},{8,9},{9,10},{10,1... | collective-permute-start | bytes 49160 | tf_op jit(solution)/shard_map/ppermute | solution.py:258
  50.0 5.0 %collective-permute-start.7 = (f32[1,128]{1,0:T(1,128)S(1)}, f32[1,128]{1,0:T(1,128)S(1)}, u32[]{:S(2)}, u32[]{:S(2)}) collective-permute-start(f32[1,128]{1,0:T(1,128)S(1)} %multiply_bitcast_fusion), channel_id=1, source_target_pairs={{0,128},{128,0},{1,129},{129,1},{2,130},{130,2},{3,131},{131,3},{4... | collective-permute-start | bytes 1544 | tf_op jit(solution)/shard_map/ppermute | solution.py:262

commit v6 on v5

--- a/solution.py
+++ b/solution.py
@@ -55,8 +55,7 @@
         rf_copy(unit).start()
     keep[...] = jnp.zeros_like(keep)
     send[...] = jnp.zeros_like(send)
-    for copy in small:
-        copy.wait()
+    small[3].wait()
     width = 2 * BLOCK
     line = jnp.concatenate(
         [
@@ -72,14 +71,6 @@
         :, :BLOCK
     ].astype(jnp.bfloat16)
 
-    columns = tiles // ROWS
-
-    def note(index, carry):
-        ahead = lax.rem(index // columns - row[0] + ROWS, ROWS)
-        place[owned[index]] = ahead * columns + lax.rem(index, columns)
-        return carry
-
-    lax.fori_loop(0, tiles, note, 0)
 
     blocks = samples // BLOCK
     units = waves * chunks
@@ -125,6 +116,14 @@
     for unit in range(2, 4):
         rf_copy(unit).start()
     lax.fori_loop(0, units // 2, two_units, 0)
+
+    for at in (0, 1, 2, 4):
+        small[at].wait()
+    columns = tiles // ROWS
+    for line_of in range(ROWS):
+        ahead = lax.rem(line_of + ROWS - row[0], ROWS) * columns
+        for index in range(columns):
+            place[owned[line_of * columns + index]] = ahead + index
 
     lane_index = lax.broadcasted_iota(jnp.int32, (frames, LANES), 1)
 

time: 55.2 us -> 55 us (level)
  starting transfers between devices: 15 us -> 16.8 us
  Pallas kernels: 11.8 us -> 10.3 us
  blocking collectives: 17.6 us -> 16.5 us
  waiting for transfers between devices: 9.75 us -> 10.5 us
    ppermute x3, starting transfers between devices: 3.89 us -> 7.05 us  [on_device(): lax.ppermute(pairs[hop], 'tile', [(i, (i + hop * columns) % tiles) for i...]
    pallas_call x1, Pallas kernels: 11.8 us -> 10.3 us  [local_images(): pl.pallas_call(beam_kernel, out_shape=(image, image), in_specs=[smem, sme...]
    ppermute x1, starting transfers between devices: 3.31 us -> 1.91 us  [on_device(): got = lax.ppermute(send, 'section', swap)]
    all_to_all x1, blocking collectives: 17.6 us -> 16.5 us  [on_device(): lax.all_to_all(line, 'tile', 0, 0, axis_index_groups=groups, tiled=True)]
    ppermute x3, waiting for transfers between devices: 4.18 us -> 4.91 us  [on_device(): lax.ppermute(pairs[hop], 'tile', [(i, (i + hop * columns) % tiles) for i...]
  transfers between devices with their start and end apart: 8 -> 8, of which waited for: 6 -> 7; matrix products, arithmetic and copies ran while one was open for 0% -> 0% of each run, Pallas kernels for 0% -> 0%
where the time goes in v6:
time: 55 us; the launch traced here: 55.4 us
  starting transfers between devices  16.8 us (31%)
  blocking collectives  16.5 us (30%)
  waiting for transfers between devices  10.5 us (19%)
  Pallas kernels  10.3 us (19%)
  between operations  0.68 us (1%)
  other arithmetic  0.67 us (1%)
    all_to_all x1, blocking collectives, on_device(): lax.all_to_all(line, 'tile', 0, 0, axis_index_groups=groups, tiled=True)  16.5 us
    pallas_call x1, Pallas kernels, local_images(): pl.pallas_call(beam_kernel, out_shape=(image, image), in_specs=[smem, sme...  10.3 us
    ppermute x3, starting transfers between devices, on_device(): lax.ppermute(pairs[hop], 'tile', [(i, (i + hop * columns) % tiles) for i...  7.05 us
    ppermute x3, waiting for transfers between devices, on_device(): lax.ppermute(pairs[hop], 'tile', [(i, (i + hop * columns) % tiles) for i...  4.91 us
    ppermute x1, starting transfers between devices, on_device(): return power + lax.ppermute(power, 'section', swap)  4.17 us
    ppermute x3, starting transfers between devices, on_device(): lax.ppermute(mine, 'wave', [(i, (i + hop) % wave_groups) for i in range(w...  3.67 us
    ppermute x3, waiting for transfers between devices, on_device(): lax.ppermute(mine, 'wave', [(i, (i + hop) % wave_groups) for i in range(w...  3.2 us
    ppermute x1, starting transfers between devices, on_device(): got = lax.ppermute(send, 'section', swap)  1.91 us
  transfers between devices with their start and end apart: 8, of which 7 were waited for; matrix products, arithmetic and copies ran while one was open for 0% of the time, Pallas kernels for 0%

profile of v6, /device:TPU:1, one launch (start us, length us, event | category | flops | bytes accessed | tf_op | source)
XLA Modules:
  0.0 55.4 jit_solution(6532287447579438041)
XLA Ops:
  0.7 10.3 %beams.1 = (f32[32,32,128]{2,1,0:T(8,128)S(1)}, f32[32,32,128]{2,1,0:T(8,128)S(1)}) custom-call(s32[1]{0:T(128)} %bitcast.side, s32[1]{0:T(128)} %bitcast.1.row, s32[1]{0:T(128)S(6)} %copy.9.live, s32[1,2,16]{2,1,0:T(2,128)} %bitcast.8, s32[1,16]{1,0:T(1,128)} %fanout_in.1, s32[32]{0:T(128)} %owned_in.1, bf16[2,64,16,2048]{3,2,1,0:T(8,128)(2,1)} %rf_in.1, ...), custom_call_target="tpu_custom_call" | custom-call | tf_op jit(solution)/shard_map/beams/pallas_call | solution.py:193
  10.9 1.9 %collective-permute-start = (f32[32,32,128]{2,1,0:T(8,128)S(1)}, f32[32,32,128]{2,1,0:T(8,128)S(1)}, u32[]{:S(2)}, u32[]{:S(2)}) collective-permute-start(f32[32,32,128]{2,1,0:T(8,128)S(1)} %get-tuple-element.8), channel_id=1, source_target_pairs={{0,128},{128,0},{1,129},{129,1},{2,130},{130,2},{3,131},{131,3},{4... | collective-permute-start | bytes 1572872 | tf_op jit(solution)/shard_map/ppermute | solution.py:242
  12.8 1.5 %collective-permute-done = f32[32,32,128]{2,1,0:T(8,128)S(1)} collective-permute-done((f32[32,32,128]{2,1,0:T(8,128)S(1)}, f32[32,32,128]{2,1,0:T(8,128)S(1)}, u32[]{:S(2)}, u32[]{:S(2)}) %collective-permute-start) | collective-permute-done | bytes 524320 | tf_op jit(solution)/shard_map/ppermute | solution.py:242
  14.4 0.1 slice_add_fusion.2
  14.4 2.2 %collective-permute-start.1 = (f32[8,32,128]{2,1,0:T(8,128)S(1)}, f32[8,32,128]{2,1,0:T(8,128)S(1)}, u32[]{:S(2)}, u32[]{:S(2)}) collective-permute-start(f32[8,32,128]{2,1,0:T(8,128)S(1)} %get-tuple-element.9), channel_id=1, source_target_pairs={{0,32},{4,36},{8,40},{12,44},{16,48},{20,52},{24,56},{28,60},{32,6... | collective-permute-start | bytes 393224 | tf_op jit(solution)/shard_map/ppermute | solution.py:249
  16.6 1.8 %collective-permute-start.3 = (f32[8,32,128]{2,1,0:T(8,128)S(1)}, f32[8,32,128]{2,1,0:T(8,128)S(1)}, u32[]{:S(2)}, u32[]{:S(2)}) collective-permute-start(f32[8,32,128]{2,1,0:T(8,128)S(1)} %get-tuple-element.10), channel_id=1, source_target_pairs={{0,96},{4,100},{8,104},{12,108},{16,112},{20,116},{24,120},{28,124... | collective-permute-start | bytes 393224 | tf_op jit(solution)/shard_map/ppermute | solution.py:249
  18.5 3.0 %collective-permute-start.2 = (f32[8,32,128]{2,1,0:T(8,128)S(1)}, f32[8,32,128]{2,1,0:T(8,128)S(1)}, u32[]{:S(2)}, u32[]{:S(2)}) collective-permute-start(f32[8,32,128]{2,1,0:T(8,128)S(1)} %get-tuple-element.11), channel_id=1, source_target_pairs={{0,64},{4,68},{8,72},{12,76},{16,80},{20,84},{24,88},{28,92},{32,9... | collective-permute-start | bytes 393224 | tf_op jit(solution)/shard_map/ppermute | solution.py:249
  21.5 0.5 collective-permute-done.1
  22.0 1.0 %collective-permute-done.3 = f32[8,32,128]{2,1,0:T(8,128)S(1)} collective-permute-done((f32[8,32,128]{2,1,0:T(8,128)S(1)}, f32[8,32,128]{2,1,0:T(8,128)S(1)}, u32[]{:S(2)}, u32[]{:S(2)}) %collective-permute-start.3) | collective-permute-done | bytes 131104 | tf_op jit(solution)/shard_map/ppermute | solution.py:249
  23.0 3.5 %collective-permute-done.2 = f32[8,32,128]{2,1,0:T(8,128)S(1)} collective-permute-done((f32[8,32,128]{2,1,0:T(8,128)S(1)}, f32[8,32,128]{2,1,0:T(8,128)S(1)}, u32[]{:S(2)}, u32[]{:S(2)}) %collective-permute-start.2) | collective-permute-done | bytes 131104 | tf_op jit(solution)/shard_map/ppermute | solution.py:249
  26.4 0.1 fusion.2
  26.5 16.5 %all_to_all.5 = f32[8,32,128]{2,1,0:T(8,128)S(1)} all-to-all(f32[8,32,128]{2,1,0:T(8,128)S(1)} %fusion.2), channel_id=1, replica_groups={{0,4,8,12,16,20,24,28},{32,36,40,44,48,52,56,60},{64,68,72,76,80,84,88,..., dimensions={0} | all-to-all | bytes 262144 | tf_op jit(solution)/shard_map/all_to_all | solution.py:253
  43.0 2.6 %collective-permute-start.6 = (f32[32,128]{1,0:T(8,128)S(1)}, f32[32,128]{1,0:T(8,128)S(1)}, u32[]{:S(2)}, u32[]{:S(2)}) collective-permute-start(f32[32,128]{1,0:T(8,128)S(1)} %reduce_sum.18), channel_id=1, source_target_pairs={{0,3},{1,0},{2,1},{3,2},{4,7},{5,4},{6,5},{7,6},{8,11},{9,8},{10,9... | collective-permute-start | bytes 49160 | tf_op jit(solution)/shard_map/ppermute | solution.py:257
  45.6 0.5 collective-permute-start.5
  46.1 0.6 %collective-permute-start.4 = (f32[32,128]{1,0:T(8,128)S(1)}, f32[32,128]{1,0:T(8,128)S(1)}, u32[]{:S(2)}, u32[]{:S(2)}) collective-permute-start(f32[32,128]{1,0:T(8,128)S(1)} %reduce_sum.18), channel_id=1, source_target_pairs={{0,1},{1,2},{2,3},{3,0},{4,5},{5,6},{6,7},{7,4},{8,9},{9,10},{10,1... | collective-permute-start | bytes 49160 | tf_op jit(solution)/shard_map/ppermute | solution.py:257
  46.7 0.0 collective-permute-done.6
  46.7 3.0 %collective-permute-done.5 = f32[32,128]{1,0:T(8,128)S(1)} collective-permute-done((f32[32,128]{1,0:T(8,128)S(1)}, f32[32,128]{1,0:T(8,128)S(1)}, u32[]{:S(2)}, u32[]{:S(2)}) %collective-permute-start.5) | collective-permute-done | bytes 16416 | tf_op jit(solution)/shard_map/ppermute | solution.py:257
  49.7 0.2 collective-permute-done.4
  49.9 4.2 %collective-permute-start.7 = (f32[1,128]{1,0:T(1,128)S(1)}, f32[1,128]{1,0:T(1,128)S(1)}, u32[]{:S(2)}, u32[]{:S(2)}) collective-permute-start(f32[1,128]{1,0:T(1,128)S(1)} %multiply_bitcast_fusion), channel_id=1, source_target_pairs={{0,128},{128,0},{1,129},{129,1},{2,130},{130,2},{3,131},{131,3},{4... | collective-permute-start | bytes 1544 | tf_op jit(solution)/shard_map/ppermute | solution.py:261
  54.1 0.8 %collective-permute-done.7 = f32[1,128]{1,0:T(1,128)S(1)} collective-permute-done((f32[1,128]{1,0:T(1,128)S(1)}, f32[1,128]{1,0:T(1,128)S(1)}, u32[]{:S(2)}, u32[]{:S(2)}) %collective-permute-start.7) | collective-permute-done | bytes 544 | tf_op jit(solution)/shard_map/ppermute | solution.py:261
  54.9 0.5 fusion.3
  (3 shorter events, 0.0 us)
Async XLA Ops:
  10.9 3.4 %collective-permute-start = (f32[32,32,128]{2,1,0:T(8,128)S(1)}, f32[32,32,128]{2,1,0:T(8,128)S(1)}, u32[]{:S(2)}, u32[]{:S(2)}) collective-permute-start(f32[32,32,128]{2,1,0:T(8,128)S(1)} %get-tuple-element.8), channel_id=1, source_target_pairs={{0,128},{128,0},{1,129},{129,1},{2,130},{130,2},{3,131},{131,3},{4... | collective-permute-start | bytes 1572872 | tf_op jit(solution)/shard_map/ppermute | solution.py:242
  14.4 7.5 %collective-permute-start.1 = (f32[8,32,128]{2,1,0:T(8,128)S(1)}, f32[8,32,128]{2,1,0:T(8,128)S(1)}, u32[]{:S(2)}, u32[]{:S(2)}) collective-permute-start(f32[8,32,128]{2,1,0:T(8,128)S(1)} %get-tuple-element.9), channel_id=1, source_target_pairs={{0,32},{4,36},{8,40},{12,44},{16,48},{20,52},{24,56},{28,60},{32,6... | collective-permute-start | bytes 393224 | tf_op jit(solution)/shard_map/ppermute | solution.py:249
  16.6 6.3 %collective-permute-start.3 = (f32[8,32,128]{2,1,0:T(8,128)S(1)}, f32[8,32,128]{2,1,0:T(8,128)S(1)}, u32[]{:S(2)}, u32[]{:S(2)}) collective-permute-start(f32[8,32,128]{2,1,0:T(8,128)S(1)} %get-tuple-element.10), channel_id=1, source_target_pairs={{0,96},{4,100},{8,104},{12,108},{16,112},{20,116},{24,120},{28,124... | collective-permute-start | bytes 393224 | tf_op jit(solution)/shard_map/ppermute | solution.py:249
  18.5 7.9 %collective-permute-start.2 = (f32[8,32,128]{2,1,0:T(8,128)S(1)}, f32[8,32,128]{2,1,0:T(8,128)S(1)}, u32[]{:S(2)}, u32[]{:S(2)}) collective-permute-start(f32[8,32,128]{2,1,0:T(8,128)S(1)} %get-tuple-element.11), channel_id=1, source_target_pairs={{0,64},{4,68},{8,72},{12,76},{16,80},{20,84},{24,88},{28,92},{32,9... | collective-permute-start | bytes 393224 | tf_op jit(solution)/shard_map/ppermute | solution.py:249
  43.0 3.7 %collective-permute-start.6 = (f32[32,128]{1,0:T(8,128)S(1)}, f32[32,128]{1,0:T(8,128)S(1)}, u32[]{:S(2)}, u32[]{:S(2)}) collective-permute-start(f32[32,128]{1,0:T(8,128)S(1)} %reduce_sum.18), channel_id=1, source_target_pairs={{0,3},{1,0},{2,1},{3,2},{4,7},{5,4},{6,5},{7,6},{8,11},{9,8},{10,9... | collective-permute-start | bytes 49160 | tf_op jit(solution)/shard_map/ppermute | solution.py:257
  45.6 4.1 %collective-permute-start.5 = (f32[32,128]{1,0:T(8,128)S(1)}, f32[32,128]{1,0:T(8,128)S(1)}, u32[]{:S(2)}, u32[]{:S(2)}) collective-permute-start(f32[32,128]{1,0:T(8,128)S(1)} %reduce_sum.18), channel_id=1, source_target_pairs={{0,2},{1,3},{2,0},{3,1},{4,6},{5,7},{6,4},{7,5},{8,10},{9,11},{10,... | collective-permute-start | bytes 49160 | tf_op jit(solution)/shard_map/ppermute | solution.py:257
  46.1 3.8 %collective-permute-start.4 = (f32[32,128]{1,0:T(8,128)S(1)}, f32[32,128]{1,0:T(8,128)S(1)}, u32[]{:S(2)}, u32[]{:S(2)}) collective-permute-start(f32[32,128]{1,0:T(8,128)S(1)} %reduce_sum.18), channel_id=1, source_target_pairs={{0,1},{1,2},{2,3},{3,0},{4,5},{5,6},{6,7},{7,4},{8,9},{9,10},{10,1... | collective-permute-start | bytes 49160 | tf_op jit(solution)/shard_map/ppermute | solution.py:257
  49.9 5.0 %collective-permute-start.7 = (f32[1,128]{1,0:T(1,128)S(1)}, f32[1,128]{1,0:T(1,128)S(1)}, u32[]{:S(2)}, u32[]{:S(2)}) collective-permute-start(f32[1,128]{1,0:T(1,128)S(1)} %multiply_bitcast_fusion), channel_id=1, source_target_pairs={{0,128},{128,0},{1,129},{129,1},{2,130},{130,2},{3,131},{131,3},{4... | collective-permute-start | bytes 1544 | tf_op jit(solution)/shard_map/ppermute | solution.py:261
